TPU v7x, 128 devices: a whole 4x4x4 slice. The times are simulated.
128 devices in a mesh: row: 8 (over z, x_hi), col: 16 (over x_lo, y, core).
Axes of the slice: x: 4 (x_hi: 2, x_lo: 2; x = x_hi * 2 + x_lo), y: 4, z: 4, core: 2. Of those that a mesh axis runs over, the one named last changes fastest.
Arguments:
- cycle_cells: int32 [2, 16384], P(None, ('row', 'col')), may hold values from 0 to 1023, as said below
- cycle_offsets: float32 [2, 16384], P(None, ('row', 'col')), may hold values from 0 to 1
- cycle_strength: float32 [16384], P(('row', 'col')), may hold values from -48 to 48
- block_tile: int32 [8192], P(('row', 'col')), may hold values from 0 to 127, as said below
Outputs:
- displacement: float32 [2, 16384], P(None, ('row', 'col'))
- diffused: float32 [4096, 8192], P('col', 'row')
- renewed: float32 [16384], P(('row', 'col'))
Inputs may be any that keep to these rules, and one draw needn't show every extreme that they name: Block b's cycles lie in the tile with slab block_tile[b] // 16 and radial part block_tile[b] mod 16. The blocks of one device name one tile at most 2 times and one slab at most 2 * 16 times; in every draw some slab is named 2 * 16 times by every device, each of its tiles twice. `cycle_cells`: row 0 is a radial cell within the cycle's tile, below 256; row 1 an axial cell, below 1024.
All inputs are finite; a program needn't handle non-finite values.
Results may differ from a plain program's by a relative error of at most 0.0004.
Values sent between devices are 32-bit elements; how exact they have to be, the bound alone decides.
A program may use at most 64 MiB of HBM per device.

v0:
```python
import math

import jax
import jax.numpy as jnp
from jax import lax
from jax.sharding import PartitionSpec as P

CR = 256
CZ = 1024
AGM_STEPS = 6


CORE_SQUARE = 4.0
STEP_LENGTH = 4.0
VISCOSITY = 0.2


def passed_along(block, axis, distance):
    devices = range(lax.axis_size(axis))
    route = [(i - distance, i) for i in devices if i - distance in devices]
    return lax.ppermute(block, axis, route)


def extended(shard, sides, width):
    for axis, dim in sides:
        peers, length = (lax.axis_size(axis), shard.shape[dim])
        up = [(i, (i + 1) % peers) for i in range(peers - 1)]
        down = [(j, i) for i, j in up]
        last = lax.slice_in_dim(shard, length - width, length, axis=dim)
        first = lax.slice_in_dim(shard, 0, width, axis=dim)
        before = lax.ppermute(last, axis, up)
        after = lax.ppermute(first, axis, down)
        shard = jnp.concatenate([before, shard, after], axis=dim)
    return shard


def tent_weight(distance):
    return jnp.maximum(1.0 - jnp.abs(distance), 0.0)


def pair_sums(targets, sources):
    target_r = targets[0][:, None]
    target_z = targets[1][:, None]
    source_r = sources[0][None, :]
    source_z = sources[1][None, :]
    source_gamma = sources[2][None, :]
    axial_gap = target_z - source_z
    smooth_sq = axial_gap * axial_gap + CORE_SQUARE
    radius_sum = target_r + source_r
    radius_gap = target_r - source_r
    far_sq = radius_sum * radius_sum + smooth_sq
    near_sq = radius_gap * radius_gap + smooth_sq
    modulus_sq = 4.0 * target_r * source_r / far_sq
    upper_mean = jnp.ones_like(far_sq)
    lower_mean = jnp.sqrt(near_sq / far_sq)
    series = 0.5 * modulus_sq
    factor = 1.0
    for agm_step in range(AGM_STEPS):
        half_gap = 0.5 * (upper_mean - lower_mean)
        upper_mean, lower_mean = (
            0.5 * (upper_mean + lower_mean),
            jnp.sqrt(upper_mean * lower_mean),
        )
        series = series + factor * half_gap * half_gap
        factor = factor * 2.0
    kind_first = 0.5 * math.pi / upper_mean
    kind_second = kind_first * (1.0 - series)
    prefactor = source_gamma / (2.0 * math.pi * jnp.sqrt(far_sq))
    square_sum = source_r * source_r + target_r * target_r + smooth_sq
    square_gap = source_r * source_r - target_r * target_r - smooth_sq
    axial_part = prefactor * (kind_first + square_gap / near_sq * kind_second)
    radial_part = (
        prefactor * axial_gap / target_r * (square_sum / near_sq * kind_second - kind_first)
    )
    return jnp.stack([jnp.sum(radial_part, axis=1), jnp.sum(axial_part, axis=1)])


def cycle_velocity(targets, sources):
    target_count = targets.shape[1]
    block_width = 512
    grouped = targets.reshape(2, target_count // block_width, block_width).transpose(1, 0, 2)
    result = lax.map(lambda target_group: pair_sums(target_group, sources), grouped)
    return result.transpose(1, 0, 2).reshape(2, target_count)


def diffuse(padded, first_row):
    center = padded[1:-1, 1:-1]
    outward = padded[2:, 1:-1]
    inward = padded[:-2, 1:-1]
    forward_z = padded[1:-1, 2:]
    backward_z = padded[1:-1, :-2]
    radius = jnp.maximum(first_row + jnp.arange(center.shape[0], dtype=jnp.int32), 1).astype(
        jnp.float32
    )[:, None]
    laplace = (
        outward
        + inward
        + forward_z
        + backward_z
        - 4.0 * center
        + (outward - inward) / (2.0 * radius)
        - center / (radius * radius)
    )
    return center + VISCOSITY * laplace


def rank_slots(group_of_block, capacity, per_block):
    block_count = group_of_block.shape[0]
    numbering = jnp.arange(block_count, dtype=jnp.int32)
    earlier = (group_of_block[:, None] == group_of_block[None, :]) & (
        numbering[None, :] < numbering[:, None]
    )
    standing = jnp.sum(earlier.astype(jnp.int32), axis=1)
    first_slot = (group_of_block * capacity + standing) * per_block
    return (first_slot[:, None] + jnp.arange(per_block, dtype=jnp.int32)[None, :]).reshape(-1)


def slot_matrix(cycle_slot, slot_total):
    return (jnp.arange(slot_total, dtype=jnp.int32)[None, :] == cycle_slot[:, None]).astype(
        jnp.float32
    )


def cycle_weights(cell, offset, anchor, total):
    grid_at = anchor + jnp.arange(total, dtype=jnp.int32)
    delta = (grid_at[:, None] - cell[None, :]).astype(jnp.float32)
    return tent_weight(offset[None, :] - delta)


def deposit_cycles(arrived, row_anchor, row_total, col_anchor, col_total):
    cycle_r = arrived[0].astype(jnp.int32)
    cycle_z = arrived[1].astype(jnp.int32)
    radial_weights = cycle_weights(cycle_r, arrived[2], row_anchor, row_total) * arrived[4][None, :]
    axial_weights = cycle_weights(cycle_z, arrived[3], col_anchor, col_total)
    return lax.dot_general(
        radial_weights,
        axial_weights,
        (((1,), (1,)), ((), ())),
        precision=lax.Precision.HIGHEST,
        preferred_element_type=jnp.float32,
    )


def sample_field(field_part, arrived, row_anchor, col_anchor):
    cycle_r = arrived[0].astype(jnp.int32)
    cycle_z = arrived[1].astype(jnp.int32)
    radial_weights = cycle_weights(cycle_r, arrived[2], row_anchor, field_part.shape[0])
    axial_weights = cycle_weights(cycle_z, arrived[3], col_anchor, field_part.shape[1])
    along_rows = jnp.dot(
        field_part,
        axial_weights,
        precision=lax.Precision.HIGHEST,
        preferred_element_type=jnp.float32,
    )
    return jnp.sum(radial_weights * along_rows, axis=0)


def on_device(cycle_cells, cycle_offsets, cycle_strength, block_tile):
    row_devices = lax.axis_size("row")
    col_devices = lax.axis_size("col")
    per_block = cycle_cells.shape[1] // block_tile.shape[0]
    cycle_tile = jnp.repeat(block_tile, per_block)
    cell_r = jnp.clip(cycle_tile % col_devices * CR + cycle_cells[0], 16, CR * col_devices - 3)
    cell_z = jnp.clip(cycle_tile // col_devices * CZ + cycle_cells[1], 2, CZ * row_devices - 3)
    positions = jnp.stack(
        [
            cell_r.astype(jnp.float32) + cycle_offsets[0],
            cell_z.astype(jnp.float32) + cycle_offsets[1],
        ]
    )
    own_sources = jnp.concatenate([positions, cycle_strength[None, :]], axis=0)
    row_targets = lax.all_gather(positions, "col", axis=1, tiled=True)
    partial_sums = cycle_velocity(
        row_targets, lax.all_gather(own_sources, "row", axis=1, tiled=True)
    )
    velocity = lax.psum_scatter(partial_sums, "col", scatter_dimension=1, tiled=True)
    displacement = STEP_LENGTH * velocity
    moved_offsets = jnp.clip(cycle_offsets + displacement, -1.0, 2.0)
    payload = jnp.stack(
        [
            cell_r.astype(jnp.float32),
            cell_z.astype(jnp.float32),
            moved_offsets[0],
            moved_offsets[1],
            cycle_strength,
        ]
    )
    row_start = lax.axis_index("col") * CR
    col_start = lax.axis_index("row") * CZ
    cycle_slot = rank_slots(block_tile // col_devices, 2 * col_devices, per_block)
    slot_table = slot_matrix(cycle_slot, row_devices * 2 * col_devices * per_block)
    outgoing = jnp.dot(
        payload, slot_table, precision=lax.Precision.HIGHEST, preferred_element_type=jnp.float32
    )
    arrived = lax.all_to_all(outgoing, "row", split_axis=1, concat_axis=1, tiled=True)
    folded_r = lax.psum_scatter(
        deposit_cycles(arrived, jnp.int32(0), CR * lax.axis_size("col"), col_start - 1, CZ + 3),
        "col",
        scatter_dimension=0,
        tiled=True,
    )
    from_next_z = passed_along(folded_r[:, 0:1], "row", -1)
    from_prev_z = passed_along(folded_r[:, CZ + 1 : CZ + 3], "row", 1)
    deposited = folded_r[:, 1 : CZ + 1]
    deposited = deposited.at[:, CZ - 1 : CZ].add(from_next_z)
    deposited = deposited.at[:, 0:2].add(from_prev_z)
    padded = extended(deposited, (("row", 1), ("col", 0)), 1)
    diffused = diffuse(padded, row_start)
    widened = extended(diffused, (("row", 1),), 2)
    values = sample_field(
        lax.all_gather(widened, "col", axis=0, tiled=True), arrived, jnp.int32(0), col_start - 2
    )
    returned = lax.all_to_all(values, "row", split_axis=0, concat_axis=0, tiled=True)
    renewed = jnp.dot(
        slot_table, returned, precision=lax.Precision.HIGHEST, preferred_element_type=jnp.float32
    )
    return (displacement, diffused, renewed)


def solution(mesh):
    in_specs = (
        P(None, ("row", "col")),
        P(None, ("row", "col")),
        P(("row", "col")),
        P(("row", "col")),
    )
    out_specs = (P(None, ("row", "col")), P("col", "row"), P(("row", "col")))
    return jax.shard_map(
        on_device, mesh=mesh, in_specs=in_specs, out_specs=out_specs, check_vma=False
    )
```

profile of v0, /device:TPU:1, one launch (start us, length us, event | category | flops | bytes accessed | tf_op | source)
XLA Modules:
  0.0 520.4 jit_solution(1767718619613536940)
XLA Ops:
  7.2 0.7 broadcast_in_dim.20
  8.1 0.8 slice_add_fusion.2
  8.9 0.7 pad_maximum_fusion.4
  9.6 27.3 %all_gather.9 = f32[3,1024]{1,0:T(4,128)S(1)} all-gather(f32[3,128]{1,0:T(4,128)S(1)} %pad_maximum_fusion.4), channel_id=1, replica_groups=mesh['row'=8,'col'=16] {'row'}, dimensions={1}, use_global_device_ids=true | all-gather | bytes 13824 | tf_op jit(solution)/shard_map/all_gather | solution.py:174
  36.8 25.9 %all_gather.10 = f32[2,2048]{1,0:T(2,128)S(1)} all-gather(f32[2,128]{1,0:T(2,128)S(1)} %pad_maximum_fusion.5), channel_id=1, replica_groups=mesh['row'=8,'col'=16] {'col'}, dimensions={1}, use_global_device_ids=true | all-gather | bytes 17408 | tf_op jit(solution)/shard_map/all_gather | solution.py:172
  62.7 39.3 %while.14 = (s32[]{:T(128)}, f32[4,2,512]{2,1,0:T(2,128)S(1)}, f32[3,1024]{1,0:T(4,128)S(1)}, f32[4,2,512]{2,1,0:T(2,128)S(1)}, f32[1,1024]{1,0:T(1,128)S(1)}, /*index=5*/s32[]{:T(128)}, s32[]{:T(128)}, s32[]{}) while((s32[]{:T(128)}, f32[4,2,512]{2,1,0:T(2,128)S(1)}, f32[3,1024]{1,0:T(4,128)S(1)}, f32[4,2,512]{2,1,0:T(2,128)S(1)}, ...), condition=%wide.region_3.4_spmd, body=%wide.region_0.3_spmd.sunk | while | flops 40895488 | bytes 75893 | solution.py:82
  62.7 9.7 %fusion.90 = (f32[512]{0:T(512)S(1)}, f32[512]{0:T(512)S(1)}) fusion(f32[512]{0:T(512)S(1)} %get-tuple-element.184, f32[1024]{0:T(1024)S(1)} %bitcast.64, f32[1024]{0:T(1024)S(1)} %bitcast.54, f32[512]{0:T(512)S(1)} %bitcast.62, f32[1024]{0:T(1024)S(1)} %bitcast.55, f32[512]{0:T(512)S(1)} %bitcast.51, f32[512]{0:T(512)S(1)} %get-tuple-element.188, ...), kind=kLoop, calls=%fused_computation.38.clone.1 | loop fusion | flops 40893440 | bytes 28672 | tf_op jit(solution)/shard_map/while/body/eval_jaxpr/reduce_sum | solution.py:75
  72.6 9.7 %fusion.90 = (f32[512]{0:T(512)S(1)}, f32[512]{0:T(512)S(1)}) fusion(f32[512]{0:T(512)S(1)} %get-tuple-element.184, f32[1024]{0:T(1024)S(1)} %bitcast.64, f32[1024]{0:T(1024)S(1)} %bitcast.54, f32[512]{0:T(512)S(1)} %bitcast.62, f32[1024]{0:T(1024)S(1)} %bitcast.55, f32[512]{0:T(512)S(1)} %bitcast.51, f32[512]{0:T(512)S(1)} %get-tuple-element.188, ...), kind=kLoop, calls=%fused_computation.38.clone.1 | loop fusion | flops 40893440 | bytes 28672 | tf_op jit(solution)/shard_map/while/body/eval_jaxpr/reduce_sum | solution.py:75
  82.4 9.7 %fusion.90 = (f32[512]{0:T(512)S(1)}, f32[512]{0:T(512)S(1)}) fusion(f32[512]{0:T(512)S(1)} %get-tuple-element.184, f32[1024]{0:T(1024)S(1)} %bitcast.64, f32[1024]{0:T(1024)S(1)} %bitcast.54, f32[512]{0:T(512)S(1)} %bitcast.62, f32[1024]{0:T(1024)S(1)} %bitcast.55, f32[512]{0:T(512)S(1)} %bitcast.51, f32[512]{0:T(512)S(1)} %get-tuple-element.188, ...), kind=kLoop, calls=%fused_computation.38.clone.1 | loop fusion | flops 40893440 | bytes 28672 | tf_op jit(solution)/shard_map/while/body/eval_jaxpr/reduce_sum | solution.py:75
  92.3 9.7 %fusion.90 = (f32[512]{0:T(512)S(1)}, f32[512]{0:T(512)S(1)}) fusion(f32[512]{0:T(512)S(1)} %get-tuple-element.184, f32[1024]{0:T(1024)S(1)} %bitcast.64, f32[1024]{0:T(1024)S(1)} %bitcast.54, f32[512]{0:T(512)S(1)} %bitcast.62, f32[1024]{0:T(1024)S(1)} %bitcast.55, f32[512]{0:T(512)S(1)} %bitcast.51, f32[512]{0:T(512)S(1)} %get-tuple-element.188, ...), kind=kLoop, calls=%fused_computation.38.clone.1 | loop fusion | flops 40893440 | bytes 28672 | tf_op jit(solution)/shard_map/while/body/eval_jaxpr/reduce_sum | solution.py:75
  102.1 1.3 copy.31
  103.9 53.8 %reduce-scatter.7.cloned.1.call-done = f32[128,2]{1,0:T(8,128)} async-done(((f32[2048,2]{1,0:T(8,128)}), f32[128,2]{1,0:T(8,128)}) %reduce-scatter.7.cloned.1.call-update) | async-done | bytes 1040
  157.7 0.9 copy.32
  159.5 0.7 reshape.303
  160.2 6.6 %all-to-all-start = ((f32[8,1,320]{2,1,0:T(1,128)}), f32[8,1,320]{2,1,0:T(1,128)S(1)}, u32[]{:S(2)}, u32[]{:S(2)}) async-start(f32[8,1,320]{2,1,0:T(1,128)} %reshape.303), calls=%async_computation | async-start | bytes 24576 | tf_op jit(solution)/shard_map/all_to_all | solution.py:195
  167.1 6.3 %all-to-all-done = f32[8,1,320]{2,1,0:T(1,128)S(1)} async-done(((f32[8,1,320]{2,1,0:T(1,128)}), f32[8,1,320]{2,1,0:T(1,128)S(1)}, u32[]{:S(2)}, u32[]{:S(2)}) %all-to-all-start) | async-done | bytes 10272 | tf_op jit(solution)/shard_map/all_to_all | solution.py:195
  173.9 0.7 reduce.34
  175.1 37.6 %fusion.25 = f32[4096,1027]{0,1:T(8,128)} fusion(f32[512]{0:T(512)S(1)} %mul.386, s32[512]{0:T(512)S(1)} %convert_element_type.62, f32[512]{0:T(512)S(1)} %sub.233, s32[512]{0:T(512)S(1)} %convert_element_type.65, s32[1027]{0:T(1024)S(1)} %iota_add_fusion.2, f32[512]{0:T(512)S(1)} %sub.241), kind=kOutput, calls=%fused_computation.45 | convolution fusion | flops 25863135232 | bytes 16840716 | tf_op jit(solution)/shard_map/dot_general | solution.py:135
  212.8 96.7 %reduce-scatter.5.cloned.1.call-done = f32[256,1027]{0,1:T(8,128)} async-done(((f32[4096,1027]{0,1:T(8,128)}), f32[256,1027]{0,1:T(8,128)}) %reduce-scatter.5.cloned.1.call-update) | async-done | bytes 1051664 | tf_op jit(solution)/shard_map/reduce_scatter | solution.py:196
  309.5 0.7 slice.190
  310.2 1.3 collective-permute-start
  312.1 0.7 slice.192
  312.8 5.5 %collective-permute-start.1 = (f32[256,2]{0,1:T(2,128)S(1)}, f32[256,2]{0,1:T(2,128)S(1)}, u32[]{:S(2)}, u32[]{:S(2)}) collective-permute-start(f32[256,2]{0,1:T(2,128)S(1)} %slice.192), channel_id=1, source_target_pairs={{0,16},{16,32},{32,48},{48,64},{64,80},{80,96},{96,112},{1,17},{17... | collective-permute-start | bytes 6152 | tf_op jit(solution)/shard_map/ppermute | solution.py:21
  318.3 1.3 slice.188
  319.6 0.7 slice_add_fusion
  321.0 5.5 %collective-permute-start.2 = (f32[256,1]{0,1:T(1,128)S(1)}, f32[256,1]{0,1:T(1,128)S(1)}, u32[]{:S(2)}, u32[]{:S(2)}) collective-permute-start(f32[256,1]{0,1:T(1,128)S(1)} %slice.193), channel_id=1, source_target_pairs={{0,16},{16,32},{32,48},{48,64},{64,80},{80,96},{96,112},{1,17},{17... | collective-permute-start | bytes 3080 | tf_op jit(solution)/shard_map/ppermute | solution.py:31
  326.6 1.3 collective-permute-start.3
  327.9 4.5 collective-permute-done.3
  332.4 0.9 concatenate.28
  333.3 0.9 fusion.82
  334.2 1.2 copy.25
  335.5 6.2 %collective-permute-start.4 = (f32[1,1026]{1,0:T(1,128)S(1)}, f32[1,1026]{1,0:T(1,128)S(1)}, u32[]{:S(2)}, u32[]{:S(2)}) collective-permute-start(f32[1,1026]{1,0:T(1,128)S(1)} %copy.25), channel_id=1, source_target_pairs={{1,0},{2,1},{3,2},{4,3},{5,4},{6,5},{7,6},{8,7},{9,8},{10,9},{11,1... | collective-permute-start | bytes 12320 | tf_op jit(solution)/shard_map/ppermute | solution.py:32
  341.9 1.9 collective-permute-start.5
  343.8 1.0 copy.26
  344.9 1.0 copy.28
  346.0 2.2 fusion.59
  348.2 6.0 %collective-permute-start.6 = (f32[256,2]{0,1:T(2,128)S(1)}, f32[256,2]{0,1:T(2,128)S(1)}, u32[]{:S(2)}, u32[]{:S(2)}) collective-permute-start(f32[256,2]{0,1:T(2,128)S(1)} %get-tuple-element.138), channel_id=1, source_target_pairs={{0,16},{16,32},{32,48},{48,64},{64,80},{80,96},{96,112},{1,17},{17... | collective-permute-start | bytes 6152 | tf_op jit(solution)/shard_map/ppermute | solution.py:31
  354.2 1.3 collective-permute-start.7
  355.5 4.5 collective-permute-done.7
  360.0 4.9 concatenate.33
  364.9 93.6 %all-gather.2.cloned.1.call-done = f32[4096,1028]{0,1:T(8,128)} async-done(((f32[256,1028]{0,1:T(8,128)}), f32[4096,1028]{0,1:T(8,128)}) %all-gather.2.cloned.1.call-update) | async-done | bytes 16842768 | tf_op jit(solution)/shard_map/all_gather | solution.py:211
  458.6 39.5 %multiply_reduce_fusion = f32[512]{0:T(512)S(1)} fusion(f32[4096,1028]{0,1:T(8,128)} %all-gather.2.cloned.1.call-done, s32[512]{0:T(512)S(1)} %convert_element_type.62, f32[512]{0:T(512)S(1)} %sub.233, s32[512]{0:T(512)S(1)} %convert_element_type.65, s32[1028]{0:T(1024)S(1)} %iota_add_fusion.1, f32[512]{0:T(512)S(1)} %sub.241), kind=kOutput, calls=%fused_computation.44 | convolution fusion | flops 25890402304 | bytes 16857104 | tf_op jit(solution)/shard_map/dot_general | solution.py:149
  498.0 0.7 all_to_all.16
  498.7 6.5 %all-to-all-start.1 = ((f32[8,64,1]{1,2,0:T(1,128)}), f32[8,64,1]{1,2,0:T(1,128)S(1)}, u32[]{:S(2)}, u32[]{:S(2)}) async-start(f32[8,64,1]{1,2,0:T(1,128)} %bitcast.14), calls=%async_computation.2 | async-start | bytes 8192 | tf_op jit(solution)/shard_map/all_to_all | solution.py:213
  505.3 1.3 copy.30
  506.6 5.2 all-to-all-done.1
  512.3 0.7 reduce.33
  513.0 0.8 convolution_bitcast_fusion
  (68 shorter events, 5.3 us)
Async XLA Ops:
  7.2 150.5 %reduce-scatter.7.cloned.1.call-start = ((), (), s32[]{:S(2)}) async-start(), calls=%async_computation.6 | async-start | bytes 1114112
  102.0 1.4 copy-start.1
  102.0 56.5 %copy-start = (f32[2,128]{1,0:T(2,128)S(1)}, f32[2,128]{1,0:T(2,128)}, u32[]{:S(2)}) copy-start(f32[2,128]{1,0:T(2,128)} %param.11) | copy-start | bytes 3076
  102.1 57.1 %copy-start.2 = (f32[128]{0:T(128)S(1)}, f32[128]{0:T(128)}, u32[]{:S(2)}) copy-start(f32[128]{0:T(128)} %param.12) | copy-start | bytes 1540
  160.2 13.2 %all-to-all-start = ((f32[8,1,320]{2,1,0:T(1,128)}), f32[8,1,320]{2,1,0:T(1,128)S(1)}, u32[]{:S(2)}, u32[]{:S(2)}) async-start(f32[8,1,320]{2,1,0:T(1,128)} %reshape.303), calls=%async_computation | async-start | bytes 24576 | tf_op jit(solution)/shard_map/all_to_all | solution.py:195
  166.9 142.6 %reduce-scatter.5.cloned.1.call-start = ((), (), s32[]{:S(2)}) async-start(), calls=%async_computation.4 | async-start | bytes 17965056 | tf_op jit(solution)/shard_map/reduce_scatter | solution.py:196
  212.8 245.8 %all-gather.2.cloned.1.call-start = ((), (), s32[]{:S(2)}) async-start(), calls=%async_computation.5 | async-start | bytes 17965056 | tf_op jit(solution)/shard_map/all_gather | solution.py:211
  310.2 9.4 %collective-permute-start = (f32[256,1]{0,1:T(1,128)S(1)}, f32[256,1]{0,1:T(1,128)S(1)}, u32[]{:S(2)}, u32[]{:S(2)}) collective-permute-start(f32[256,1]{0,1:T(1,128)S(1)} %slice.190), channel_id=1, source_target_pairs={{16,0},{32,16},{48,32},{64,48},{80,64},{96,80},{112,96},{17,1},{33... | collective-permute-start | bytes 3080 | tf_op jit(solution)/shard_map/ppermute | solution.py:21
  312.8 7.5 %collective-permute-start.1 = (f32[256,2]{0,1:T(2,128)S(1)}, f32[256,2]{0,1:T(2,128)S(1)}, u32[]{:S(2)}, u32[]{:S(2)}) collective-permute-start(f32[256,2]{0,1:T(2,128)S(1)} %slice.192), channel_id=1, source_target_pairs={{0,16},{16,32},{32,48},{48,64},{64,80},{80,96},{96,112},{1,17},{17... | collective-permute-start | bytes 6152 | tf_op jit(solution)/shard_map/ppermute | solution.py:21
  321.0 6.8 %collective-permute-start.2 = (f32[256,1]{0,1:T(1,128)S(1)}, f32[256,1]{0,1:T(1,128)S(1)}, u32[]{:S(2)}, u32[]{:S(2)}) collective-permute-start(f32[256,1]{0,1:T(1,128)S(1)} %slice.193), channel_id=1, source_target_pairs={{0,16},{16,32},{32,48},{48,64},{64,80},{80,96},{96,112},{1,17},{17... | collective-permute-start | bytes 3080 | tf_op jit(solution)/shard_map/ppermute | solution.py:31
  326.6 5.8 %collective-permute-start.3 = (f32[256,1]{0,1:T(1,128)S(1)}, f32[256,1]{0,1:T(1,128)S(1)}, u32[]{:S(2)}, u32[]{:S(2)}) collective-permute-start(f32[256,1]{0,1:T(1,128)S(1)} %slice.194), channel_id=1, source_target_pairs={{16,0},{32,16},{48,32},{64,48},{80,64},{96,80},{112,96},{17,1},{33... | collective-permute-start | bytes 3080 | tf_op jit(solution)/shard_map/ppermute | solution.py:32
  335.5 8.3 %collective-permute-start.4 = (f32[1,1026]{1,0:T(1,128)S(1)}, f32[1,1026]{1,0:T(1,128)S(1)}, u32[]{:S(2)}, u32[]{:S(2)}) collective-permute-start(f32[1,1026]{1,0:T(1,128)S(1)} %copy.25), channel_id=1, source_target_pairs={{1,0},{2,1},{3,2},{4,3},{5,4},{6,5},{7,6},{8,7},{9,8},{10,9},{11,1... | collective-permute-start | bytes 12320 | tf_op jit(solution)/shard_map/ppermute | solution.py:32
  341.9 3.1 collective-permute-start.5
  348.2 7.4 %collective-permute-start.6 = (f32[256,2]{0,1:T(2,128)S(1)}, f32[256,2]{0,1:T(2,128)S(1)}, u32[]{:S(2)}, u32[]{:S(2)}) collective-permute-start(f32[256,2]{0,1:T(2,128)S(1)} %get-tuple-element.138), channel_id=1, source_target_pairs={{0,16},{16,32},{32,48},{48,64},{64,80},{80,96},{96,112},{1,17},{17... | collective-permute-start | bytes 6152 | tf_op jit(solution)/shard_map/ppermute | solution.py:31
  354.2 5.8 %collective-permute-start.7 = (f32[256,2]{0,1:T(2,128)S(1)}, f32[256,2]{0,1:T(2,128)S(1)}, u32[]{:S(2)}, u32[]{:S(2)}) collective-permute-start(f32[256,2]{0,1:T(2,128)S(1)} %get-tuple-element.137), channel_id=1, source_target_pairs={{16,0},{32,16},{48,32},{64,48},{80,64},{96,80},{112,96},{17,1},{33... | collective-permute-start | bytes 6152 | tf_op jit(solution)/shard_map/ppermute | solution.py:32
  498.7 13.1 %all-to-all-start.1 = ((f32[8,64,1]{1,2,0:T(1,128)}), f32[8,64,1]{1,2,0:T(1,128)S(1)}, u32[]{:S(2)}, u32[]{:S(2)}) async-start(f32[8,64,1]{1,2,0:T(1,128)} %bitcast.14), calls=%async_computation.2 | async-start | bytes 8192 | tf_op jit(solution)/shard_map/all_to_all | solution.py:213
Sparse Core Ops, SparseCore 0:
  103.6 54.0 reduce-scatter.6
  212.9 96.5 reduce-scatter.4
  365.1 93.4 all-gather.1
where the time goes:
time: 522 us; the launch traced here: 520 us
  waiting for transfers between devices  265 us (51%)
  matrix products  78.1 us (15%)
  blocking collectives  53.1 us (10%)
  other arithmetic  47 us (9%)
  starting transfers between devices  42.5 us (8%)
  local copies, waits for them, and re-layouts  20.7 us (4%)
  between operations  14 us (3%)
    reduce_scatter x1, waiting for transfers between devices, on_device(): lax.psum_scatter(deposit_cycles(arrived, jnp.int32(0), CR * lax.axis_size...  96.7 us
    all_gather x1, waiting for transfers between devices, on_device(): lax.all_gather(widened, 'col', axis=0, tiled=True)  93.6 us
    unnamed x4, waiting for transfers between devices  53.8 us
    dot_general x1, matrix products, sample_field(): jnp.dot(field_part, axial_weights, precision=lax.Precision.HIGHEST, prefe...  39.5 us
    reduce_sum x4, other arithmetic, pair_sums(): jnp.sum(radial_part, axis=1)  39 us
    dot_general x1, matrix products, deposit_cycles(): lax.dot_general(radial_weights, axial_weights, (((1,), (1,)), ((), ())),...  37.6 us
    all_gather x1, blocking collectives, on_device(): lax.all_gather(own_sources, 'row', axis=1, tiled=True)  27.3 us
    all_gather x1, blocking collectives, on_device(): row_targets = lax.all_gather(positions, 'col', axis=1, tiled=True)  25.9 us
  transfers between devices with their start and end apart: 13, of which 8 were waited for; matrix products, arithmetic and copies ran while one was open for 1% of the time, Pallas kernels for 0%

commit v1 on v0

v1 whole, which is shorter than its diff:
```python
import jax
import jax.numpy as jnp
from jax import lax
from jax.experimental import pallas as pl
from jax.experimental.pallas import tpu as pltpu
from jax.sharding import PartitionSpec as P

MESH = pl.DeviceIdType.MESH
F32 = jnp.float32
BF16 = jnp.bfloat16
HIGH = lax.Precision.HIGHEST

N_ROW = 8
N_COL = 16
DEVICES = N_ROW * N_COL
CYC = 128
CR = 256
CZ = 1024
EXT_R = 264
EXT_Z = 1152
ROWS = 280
SLOTS = 512
VISCOSITY = 0.2
CORE_SQUARE = 4.0
STEP_LENGTH = 4.0
CHUNK = 16


def iota(shape, dim):
    return lax.broadcasted_iota(jnp.int32, shape, dim)


def dot(a, b, contract, precision=None):
    return lax.dot_general(
        a, b, (contract, ((), ())), precision=precision, preferred_element_type=F32
    )


def halves(x):
    high = x.astype(BF16)
    return high, (x - high.astype(F32)).astype(BF16)


def dot3(a, b, contract):
    (ah, al), (bh, bl) = a, b
    return dot(ah, bh, contract) + (dot(ah, bl, contract) + dot(al, bh, contract))


def tent(x):
    return jnp.maximum(1.0 - jnp.abs(x), 0.0)


def pair_terms(r, rr, z, a, a2, aa, src_z):
    d = z - src_z
    gap = a - r
    s = d * d + CORE_SQUARE
    near = s + gap * gap
    w = a2 * r
    u = near + w
    pq = (u + w) * near
    g = pq * lax.rsqrt(pq)
    b = g * lax.rsqrt(g)
    x = (u + g) * 0.5
    a = x * lax.rsqrt(x)
    t = []
    for _ in range(4):
        product = a * b
        t.append(product)
        a = (a + b) * 0.5
        b = product * lax.rsqrt(product)
    twice = a + b
    h = t[3]
    for n in (2, 1, 0):
        h = (h + h) + t[n]
    e = (8.0 * twice) * twice - ((h + h) + g)
    inverse = 1.0 / twice
    y = (e * inverse) * (1.0 / pq)
    radial = (u * y - inverse) * d
    even = inverse - y * s
    odd = y * (aa - rr)
    return radial, even + odd, even - odd


def kernel(
    cells_ref, offs_ref, stren_ref, btile_ref,
    disp_ref, diff_ref, renew_ref,
    src, ag, ret_send, ret_recv, tr, tz, tg, trr, acc_rad, acc_ax,
    out1, in1, out2, in2, rv, zf, zh, zl, ns_send, ns_recv, ew_send, ew_recv, co_recv, dep, fld,
    ag_ssem, ag_rsem, ret_sem, a1_sem, halo_ssem, halo_rsem, a2_sem,
):
    row = lax.axis_index("row")
    col = lax.axis_index("col")

    def at(kr, kc):
        return lax.rem(row + kr, N_ROW), lax.rem(col + kc, N_COL)

    def before(kr, kc):
        return lax.rem(row + (N_ROW - kr), N_ROW), lax.rem(col + (N_COL - kc), N_COL)

    def each_shift(body):
        def first(i, carry):
            body(0, 1 + i, True)
            return carry

        def middle(i, carry):
            body(1 + i // N_COL, lax.rem(i, N_COL), True)
            return carry

        def last(i, carry):
            body(4, 1 + i, True)
            return carry

        def alone(i, carry):
            body(4 * lax.rem(i, 2), 8 * (1 - i // 2), False)
            return carry

        lax.fori_loop(0, 7, first, 0)
        lax.fori_loop(0, 48, middle, 0)
        lax.fori_loop(0, 7, last, 0)
        lax.fori_loop(0, 2, alone, 0)
        body(4, 0, False)

    barrier = pltpu.get_barrier_semaphore()

    def greet(kr, kc, _):
        pl.semaphore_signal(barrier, inc=1, device_id=at(kr, kc), device_id_type=MESH)

    each_shift(greet)

    widen = (iota((64, CYC), 1) // 2 == iota((64, CYC), 0)).astype(F32)
    tile_of = dot(
        jnp.broadcast_to(btile_ref[...].astype(F32), (8, 64)), widen, ((1,), (0,)), HIGH
    )[0:1]
    tile_row = tile_of.astype(jnp.int32)
    part = tile_row & (N_COL - 1)
    slab = tile_row >> 4
    cell_r = jnp.clip(part * CR + cells_ref[0:1], 16, CR * N_COL - 3)
    cell_z = jnp.clip(slab * CZ + cells_ref[1:2], 2, CZ * N_ROW - 3)
    offs = offs_ref[...]
    pos_r = cell_r.astype(F32) + offs[0:1]
    pos_z = cell_z.astype(F32) + offs[1:2]
    strength = stren_ref[...]
    src[0:1] = pos_r
    src[1:2] = pos_z
    src[2:3] = (STEP_LENGTH * 0.5) * strength
    src[3:4] = jnp.zeros((1, CYC), F32)

    pl.semaphore_wait(barrier, 65)

    def send_source(kr, kc, _):
        pltpu.make_async_remote_copy(
            src_ref=src,
            dst_ref=ag.at[kr, kc],
            send_sem=ag_ssem,
            recv_sem=ag_rsem.at[kr, kc],
            device_id=before(kr, kc),
            device_id_type=MESH,
        ).start()

    each_shift(send_source)

    def column(v):
        return jnp.transpose(jnp.broadcast_to(v, (CYC, CYC)))

    tr[...] = column(pos_r)
    tz[...] = column(pos_z)
    tg[...] = column((STEP_LENGTH * 0.5) * strength)
    trr[...] = tr[...] * tr[...]
    acc_rad[...] = jnp.zeros((CYC, CYC), F32)
    acc_ax[...] = jnp.zeros((CYC, CYC), F32)

    def block(ref):
        a = ref[0:1, :]
        src_z = ref[1:2, :]
        src_g = ref[2:3, :]
        a, a2, aa, src_z, src_g = (
            jnp.broadcast_to(v, (CHUNK, CYC)) for v in (a, a + a, a * a, src_z, src_g)
        )
        back_rad = jnp.zeros((CHUNK, CYC), F32)
        back_ax = jnp.zeros((CHUNK, CYC), F32)
        for i in range(CYC // CHUNK):
            rows = pl.ds(i * CHUNK, CHUNK)
            radial, here, there = pair_terms(tr[rows], trr[rows], tz[rows], a, a2, aa, src_z)
            acc_rad[rows] += radial * src_g
            acc_ax[rows] += here * src_g
            own = tg[rows]
            back_rad += radial * own
            back_ax += there * own
        return back_rad, back_ax

    block(src)

    def meet(kr, kc, both):
        pltpu.make_async_copy(src, ag.at[kr, kc], ag_rsem.at[kr, kc]).wait()
        back_rad, back_ax = block(ag.at[kr, kc])
        if both:
            ret_send[kr, kc, 0:1] = jnp.sum(back_rad, axis=0, keepdims=True)
            ret_send[kr, kc, 1:2] = jnp.sum(back_ax, axis=0, keepdims=True)
            pltpu.make_async_remote_copy(
                src_ref=ret_send.at[kr, kc],
                dst_ref=ret_recv.at[kr, kc],
                send_sem=ret_sem.at[0],
                recv_sem=ret_sem.at[1],
                device_id=at(kr, kc),
                device_id_type=MESH,
            ).start()

    each_shift(meet)

    def wait_bytes(ref, count, sem):
        view = ref.at[pl.ds(0, count)]
        pltpu.make_async_copy(view, view, sem).wait()

    lane = iota((CYC, CYC), 1)
    sub = iota((CYC, CYC), 0)
    tile_rows = jnp.broadcast_to(tile_of, (CYC, CYC))
    same = (jnp.transpose(tile_rows) == tile_rows) & ((sub >> 1) < (lane >> 1))
    rank = jnp.sum(same.astype(F32), axis=0, keepdims=True)
    slot = rank.astype(jnp.int32) + (iota((1, CYC), 1) & 1)
    route = (sub == jnp.broadcast_to(tile_row, (CYC, CYC))).astype(F32)

    own_rad = jnp.sum(jnp.transpose(acc_rad[...]), axis=0, keepdims=True)
    own_ax = jnp.sum(jnp.transpose(acc_ax[...]), axis=0, keepdims=True)

    flat = ret_recv.reshape(5 * N_COL, 2, CYC)
    wait_bytes(flat, 62, ret_sem.at[1])
    got = jnp.sum(ret_recv[1:4], axis=(0, 1))
    got += jnp.sum(ret_recv[0, 1:8], axis=0) + jnp.sum(ret_recv[4, 1:8], axis=0)
    disp_r = (own_rad - got[0:1]) / pos_r
    disp_z = own_ax + got[1:2]
    disp_ref[0:1] = disp_r
    disp_ref[1:2] = disp_z

    moved_r = jnp.clip(offs[0:1] + disp_r, -1.0, 2.0)
    moved_z = jnp.clip(offs[1:2] + disp_z, -1.0, 2.0)
    local_r = (cell_r - part * CR).astype(F32)
    local_z = (cell_z - slab * CZ).astype(F32)
    blank = jnp.zeros((3, CYC), F32)
    values = jnp.concatenate([local_r, moved_r, local_z, moved_z, strength, blank], axis=0)
    payload = jnp.concatenate([jnp.where(slot == s, values, 0.0) for s in range(4)], axis=0)
    payload = jnp.concatenate([payload, jnp.zeros((96, CYC), F32)], axis=0)
    out1[:, 0, :] = dot(route, payload, ((1,), (1,)), HIGH)

    me = row * N_COL + col

    def to_all(out, into, sem):
        def outer(kr, carry):
            dr = lax.rem(row + kr, N_ROW)

            def send(dc):
                pltpu.make_async_remote_copy(
                    src_ref=out.at[dr * N_COL + dc],
                    dst_ref=into.at[me],
                    send_sem=sem.at[0],
                    recv_sem=sem.at[1],
                    device_id=(dr, dc),
                    device_id_type=MESH,
                ).start()

            for kc in range(1, N_COL):
                send(lax.rem(col + kc, N_COL))

            @pl.when(kr > 0)
            def _():
                send(col)

            return carry

        lax.fori_loop(0, N_ROW, outer, 0)
        into[me] = out[me]
        wait_bytes(into, DEVICES - 1, sem.at[1])

    to_all(out1, in1, a1_sem)

    rv[...] = in1[:, 0, :]
    across = jnp.transpose(rv[...])
    step = iota((ROWS, CYC), 0)
    wrapped = (iota((ROWS, CYC), 0) & 7) - jnp.where((iota((ROWS, CYC), 0) & 7) < 4, 0, 8)
    cell_of_row = jnp.where(
        step < 260,
        step,
        jnp.where(step < 264, step - 264, jnp.where(step < 272, CR + wrapped, wrapped)),
    ).astype(F32)
    radial = []
    for s in range(4):
        radial.append(tent((cell_of_row - across[8 * s : 8 * s + 1]) - across[8 * s + 1 : 8 * s + 2]))
    radial = jnp.concatenate(radial, axis=1)
    power = jnp.concatenate([across[8 * s + 4 : 8 * s + 5] for s in range(4)], axis=1)
    loaded = halves(radial * power)

    edge = iota((16, CYC), 0) & 7
    edge = edge - jnp.where(edge < 4, 0, 8) + jnp.where(iota((16, CYC), 0) < 8, CZ, 0)
    edge = edge.astype(F32)
    axial_edge = jnp.concatenate(
        [
            tent((edge - across[8 * s + 2 : 8 * s + 3]) - across[8 * s + 3 : 8 * s + 4])
            for s in range(4)
        ],
        axis=1,
    )
    strips = dot3(halves(axial_edge), loaded, ((1,), (1,)))
    ew_send[...] = jnp.zeros((2, 8, 384), F32)
    ew_send[0, :, 0:ROWS] = strips[0:8]
    ew_send[1, :, 0:ROWS] = strips[8:16]

    next_r, prev_r = lax.rem(row + 1, N_ROW), lax.rem(row + N_ROW - 1, N_ROW)
    next_c, prev_c = lax.rem(col + 1, N_COL), lax.rem(col + N_COL - 1, N_COL)
    copies = []

    def give(source, target, device):
        i = len(copies)
        copy = pltpu.make_async_remote_copy(
            src_ref=source,
            dst_ref=target,
            send_sem=halo_ssem.at[i],
            recv_sem=halo_rsem.at[i],
            device_id=device,
            device_id_type=MESH,
        )
        copy.start()
        copies.append(copy)

    give(ew_send.at[0], ew_recv.at[0], (next_r, col))
    give(ew_send.at[1], ew_recv.at[1], (prev_r, col))
    give(ew_send.at[0, :, pl.ds(256, 128)], co_recv.at[0], (next_r, next_c))
    give(ew_send.at[0, :, pl.ds(256, 128)], co_recv.at[1], (next_r, prev_c))
    give(ew_send.at[1, :, pl.ds(256, 128)], co_recv.at[2], (prev_r, next_c))
    give(ew_send.at[1, :, pl.ds(256, 128)], co_recv.at[3], (prev_r, prev_c))

    cell_of_lane = iota((16, EXT_Z), 1)
    cell_of_lane = jnp.where(cell_of_lane < 1088, cell_of_lane, cell_of_lane - EXT_Z).astype(F32)

    for s in range(4):

        def axial(i, carry):
            rows = pl.ds(pl.multiple_of(i * 16, 16), 16)
            into = pl.ds(pl.multiple_of(s * CYC + i * 16, 16), 16)
            one = rv[rows, :]
            w = tent((cell_of_lane - one[:, 8 * s + 2 : 8 * s + 3]) - one[:, 8 * s + 3 : 8 * s + 4])
            high, low = halves(w)
            zh[into] = high
            zl[into] = low
            return carry

        lax.fori_loop(0, 8, axial, 0)

    loaded_h, loaded_l = loaded
    along = ((1,), (0,))
    ends = dot3((loaded_h[EXT_R:], loaded_l[EXT_R:]), (zh[...], zl[...]), along)
    ns_send[0] = ends[0:8]
    ns_send[1] = ends[8:16]
    give(ns_send.at[0], ns_recv.at[0], (row, next_c))
    give(ns_send.at[1], ns_recv.at[1], (row, prev_c))

    dep[...] = dot3((loaded_h[:EXT_R], loaded_l[:EXT_R]), (zh[...], zl[...]), along)

    for copy in copies:
        copy.wait_recv()

    has_next_r, has_prev_r = row < N_ROW - 1, row > 0
    has_next_c, has_prev_c = col < N_COL - 1, col > 0
    strip_lane = iota((8, CYC), 1)

    def side(i, present):
        wide = jnp.where(present, ew_recv[i], 0.0)
        first, second, third = wide[:, 0:128], wide[:, 128:256], wide[:, 256:384]
        third = jnp.where(strip_lane < 8, third, 0.0)
        low = jnp.where(has_prev_c & present, pltpu.roll(co_recv[2 * i], 120, axis=1), 0.0)
        high = jnp.where(has_next_c & present, co_recv[2 * i + 1], 0.0)
        first += jnp.where(strip_lane < 4, low, 0.0)
        third += jnp.where((strip_lane >= 4) & (strip_lane < 8), low, 0.0)
        third += jnp.where(strip_lane < 4, pltpu.roll(high, 112, axis=1), 0.0)
        second += jnp.where(strip_lane >= 124, pltpu.roll(high, 104, axis=1), 0.0)
        wide = jnp.concatenate([first, second, third], axis=1)
        upper = iota((8, 384), 0) < 4
        wide = jnp.concatenate(
            [jnp.where(upper, wide, 0.0), jnp.zeros((112, 384), F32), jnp.where(upper, 0.0, wide)],
            axis=0,
        )
        return jnp.transpose(wide)[0:EXT_R]

    left = side(0, has_prev_r)
    right = side(1, has_next_r)
    front = iota((EXT_R, 128), 1) < 64
    dep[:, 0:128] += jnp.where(front, left, 0.0)
    dep[:, 896:1024] += jnp.where(front, 0.0, right)
    dep[:, 1024:1152] += jnp.where(front, right, left)
    upper = iota((8, EXT_Z), 0) < 4
    above = jnp.where(has_prev_c, ns_recv[0], 0.0)
    below = jnp.where(has_next_c, ns_recv[1], 0.0)
    dep[0:8] += jnp.where(upper, above, 0.0)
    dep[248:256] += jnp.where(upper, 0.0, below)
    dep[256:264] += jnp.where(upper, below, above)

    base = col * CR
    for i in range(EXT_R // 8):
        here = dep[8 * i : 8 * i + 8]
        prev = dep[8 * i - 8 : 8 * i] if i else dep[EXT_R - 8 : EXT_R]
        nxt = dep[8 * i + 8 : 8 * i + 16] if i < EXT_R // 8 - 1 else dep[0:8]
        inward = jnp.concatenate([prev[7:8], here[0:7]], axis=0)
        outward = jnp.concatenate([here[1:8], nxt[0:1]], axis=0)
        forward = pltpu.roll(here, EXT_Z - 1, axis=1)
        backward = pltpu.roll(here, 1, axis=1)
        number = iota((8, 128), 0) + 8 * i
        number = jnp.where(number < 260, number, number - EXT_R) + base
        radius = jnp.maximum(number, 1).astype(F32)
        half = jnp.concatenate([0.5 / radius] * 9, axis=1)
        square = jnp.concatenate([1.0 / (radius * radius)] * 9, axis=1)
        laplace = (
            (outward + inward)
            + (forward + backward)
            - 4.0 * here
            + (outward - inward) * half
            - here * square
        )
        new = here + VISCOSITY * laplace
        fld[8 * i : 8 * i + 8] = new
        if i < CR // 8:
            diff_ref[8 * i : 8 * i + 8] = new[:, 0:CZ]

    read = dot3(halves(fld[...]), (zh[...], zl[...]), ((1,), (1,)))
    found = jnp.sum(read * radial[:EXT_R], axis=0, keepdims=True)
    found = jnp.concatenate(
        [found[:, CYC * s : CYC * s + CYC] for s in range(4)] + [jnp.zeros((124, CYC), F32)], axis=0
    )
    out2[:, 0, :] = jnp.transpose(found)
    to_all(out2, in2, a2_sem)
    table = jnp.transpose(in2[:, 0, :])[0:8]
    mine = dot(table, route, ((1,), (0,)), HIGH)
    renew_ref[...] = jnp.sum(
        jnp.where(iota((8, CYC), 0) == slot, mine, 0.0), axis=0, keepdims=True
    )

    sent = ag.reshape(5 * N_COL, 4, CYC)
    wait_bytes(sent, 65, ag_ssem)
    wait_bytes(flat, 62, ret_sem.at[0])
    wait_bytes(out1, DEVICES - 1, a1_sem.at[0])
    wait_bytes(out2, DEVICES - 1, a2_sem.at[0])
    for copy in copies:
        copy.wait_send()


def on_device(cycle_cells, cycle_offsets, cycle_strength, block_tile):
    vmem = pl.BlockSpec(memory_space=pltpu.VMEM)
    dma = pltpu.SemaphoreType.DMA
    displacement, diffused, renewed = pl.pallas_call(
        kernel,
        out_shape=[
            jax.ShapeDtypeStruct((2, CYC), F32),
            jax.ShapeDtypeStruct((CR, CZ), F32),
            jax.ShapeDtypeStruct((1, CYC), F32),
        ],
        in_specs=[vmem] * 4,
        out_specs=[vmem] * 3,
        scratch_shapes=[
            pltpu.VMEM((4, CYC), F32),
            pltpu.VMEM((5, N_COL, 4, CYC), F32),
            pltpu.VMEM((5, N_COL, 2, CYC), F32),
            pltpu.VMEM((5, N_COL, 2, CYC), F32),
            pltpu.VMEM((CYC, CYC), F32),
            pltpu.VMEM((CYC, CYC), F32),
            pltpu.VMEM((CYC, CYC), F32),
            pltpu.VMEM((CYC, CYC), F32),
            pltpu.VMEM((CYC, CYC), F32),
            pltpu.VMEM((CYC, CYC), F32),
            pltpu.VMEM((DEVICES, 1, CYC), F32),
            pltpu.VMEM((DEVICES, 1, CYC), F32),
            pltpu.VMEM((DEVICES, 1, CYC), F32),
            pltpu.VMEM((DEVICES, 1, CYC), F32),
            pltpu.VMEM((CYC, CYC), F32),
            pltpu.VMEM((8, 128), F32),
            pltpu.VMEM((SLOTS, EXT_Z), BF16),
            pltpu.VMEM((SLOTS, EXT_Z), BF16),
            pltpu.VMEM((2, 8, EXT_Z), F32),
            pltpu.VMEM((2, 8, EXT_Z), F32),
            pltpu.VMEM((2, 8, 384), F32),
            pltpu.VMEM((2, 8, 384), F32),
            pltpu.VMEM((4, 8, 128), F32),
            pltpu.VMEM((EXT_R, EXT_Z), F32),
            pltpu.VMEM((EXT_R, EXT_Z), F32),
            dma,
            dma((5, N_COL)),
            dma((2,)),
            dma((2,)),
            dma((8,)),
            dma((8,)),
            dma((2,)),
        ],
        compiler_params=pltpu.CompilerParams(
            collective_id=0, has_side_effects=True, vmem_limit_bytes=48 * 2**20
        ),
    )(cycle_cells, cycle_offsets, cycle_strength.reshape(1, CYC), block_tile.reshape(1, -1))
    return displacement, diffused, renewed.reshape(CYC)


def solution(mesh):
    in_specs = (
        P(None, ("row", "col")),
        P(None, ("row", "col")),
        P(("row", "col")),
        P(("row", "col")),
    )
    out_specs = (P(None, ("row", "col")), P("col", "row"), P(("row", "col")))
    return jax.shard_map(
        on_device, mesh=mesh, in_specs=in_specs, out_specs=out_specs, check_vma=False
    )
```

time: 522 us -> 58.8 us (0.11)
  waiting for transfers between devices: 265 us -> 0 us
  matrix products: 78.1 us -> 0 us
  Pallas kernels: 0 us -> 55.2 us
  blocking collectives: 53.1 us -> 0 us
  other arithmetic: 47 us -> 0 us
  starting transfers between devices: 42.5 us -> 0 us
  local copies, waits for them, and re-layouts: 20.7 us -> 2.73 us
  between operations: 14 us -> 0.67 us
    reduce_scatter x1 -> x0, waiting for transfers between devices: 96.7 us -> none  [on_device(): lax.psum_scatter(deposit_cycles(arrived, jnp.int32(0), CR * lax.axis_size...]
    all_gather x1 -> x0, waiting for transfers between devices: 93.6 us -> none  [on_device(): lax.all_gather(widened, 'col', axis=0, tiled=True)]
    dot_general x4 -> x0, matrix products: 78.1 us -> none  [the longest x1 39.5 us: sample_field(): jnp.dot(field_part, axial_weights, precision=lax.Precision.HIGHEST, prefe...]
    pallas_call x0 -> x1, Pallas kernels: none -> 55.2 us  [on_device(): pl.pallas_call(kernel, out_shape=[jax.ShapeDtypeStruct((2, CYC), F32), ja...]
    unnamed x4 -> x0, waiting for transfers between devices: 53.8 us -> none
    all_gather x2 -> x0, blocking collectives: 53.1 us -> none  [the longest x1 27.3 us: on_device(): lax.all_gather(own_sources, 'row', axis=1, tiled=True)]
    reduce_sum x5 -> x0, other arithmetic: 39.2 us -> none  [the longest x4 39 us: pair_sums(): jnp.sum(radial_part, axis=1)]
    ppermute x8 -> x0, starting transfers between devices: 29 us -> none  [the longest x3 13.5 us: extended(): before = lax.ppermute(last, axis, up)]
  transfers between devices with their start and end apart: 13 -> 0, of which waited for: 8 -> 0; matrix products, arithmetic and copies ran while one was open for 1% -> 0% of each run, Pallas kernels for 0% -> 0%
where the time goes in v1:
time: 58.8 us; the launch traced here: 58.6 us
  Pallas kernels  55.2 us (94%)
  local copies, waits for them, and re-layouts  2.73 us (5%)
  between operations  0.67 us (1%)
    pallas_call x1, Pallas kernels, on_device(): pl.pallas_call(kernel, out_shape=[jax.ShapeDtypeStruct((2, CYC), F32), ja...  55.2 us
    unnamed x11, local copies, waits for them, and re-layouts  2.73 us

profile of v1, /device:TPU:1, one launch (start us, length us, event | category | flops | bytes accessed | tf_op | source)
XLA Modules:
  0.0 58.6 jit_solution(3546363285940041639)
XLA Ops:
  0.6 0.0 copy-start.1
  0.6 0.0 copy-start.3
  0.7 0.0 copy-start
  0.7 0.0 copy-start.2
  0.7 0.6 %copy-done.1 = f32[2,128]{1,0:T(2,128)S(1)} copy-done((f32[2,128]{1,0:T(2,128)S(1)}, f32[2,128]{1,0:T(2,128)}, u32[]{:S(2)}) %copy-start.1) | copy-done | bytes 1048
  1.3 0.0 copy-done.3
  1.3 0.0 copy-done
  1.3 0.0 copy-done.2
  1.3 55.2 %shard_map.67 = (f32[2,128]{1,0:T(2,128)S(1)}, f32[256,1024]{1,0:T(8,128)S(1)}, f32[1,128]{1,0:T(1,128)S(1)}) custom-call(s32[2,128]{1,0:T(2,128)S(1)} %copy-done, f32[2,128]{1,0:T(2,128)S(1)} %copy-done.1, f32[1,128]{1,0:T(1,128)S(1)} %bitcast.3, s32[1,64]{1,0:T(1,128)S(1)} %bitcast.4), custom_call_target="tpu_custom_call" | custom-call | tf_op jit(solution)/shard_map/pallas_call | solution.py:446
  56.6 0.6 copy.10
  57.2 1.0 %copy.11 = f32[256,1024]{1,0:T(8,128)} copy(f32[256,1024]{1,0:T(8,128)S(1)} %get-tuple-element.13) | data formatting | bytes 2097152
  58.1 0.5 copy.12
Async XLA Ops:
  0.6 0.7 %copy-start.1 = (f32[2,128]{1,0:T(2,128)S(1)}, f32[2,128]{1,0:T(2,128)}, u32[]{:S(2)}) copy-start(f32[2,128]{1,0:T(2,128)} %offs_ref.1) | copy-start | bytes 3076
  0.6 0.7 %copy-start.3 = (s32[64]{0:T(128)S(1)}, s32[64]{0:T(128)}, u32[]{:S(2)}) copy-start(s32[64]{0:T(128)} %param.7) | copy-start | bytes 772
  0.7 0.7 %copy-start = (s32[2,128]{1,0:T(2,128)S(1)}, s32[2,128]{1,0:T(2,128)}, u32[]{:S(2)}) copy-start(s32[2,128]{1,0:T(2,128)} %cells_ref.1) | copy-start | bytes 3076
  0.7 0.7 %copy-start.2 = (f32[128]{0:T(128)S(1)}, f32[128]{0:T(128)}, u32[]{:S(2)}) copy-start(f32[128]{0:T(128)} %param.6) | copy-start | bytes 1540

commit v2 on v1

--- a/solution.py
+++ b/solution.py
@@ -23,7 +23,7 @@
 VISCOSITY = 0.2
 CORE_SQUARE = 4.0
 STEP_LENGTH = 4.0
-CHUNK = 16
+CHUNK = 128
 
 
 def iota(shape, dim):
@@ -82,11 +82,12 @@
 
 
 def kernel(
-    cells_ref, offs_ref, stren_ref, btile_ref,
-    disp_ref, diff_ref, renew_ref,
+    cells_hbm, offs_hbm, stren_hbm, btile_hbm,
+    disp_out, diff_out, renew_out,
+    cells_ref, offs_ref, stren_ref, btile_ref, disp_ref, renew_ref,
     src, ag, ret_send, ret_recv, tr, tz, tg, trr, acc_rad, acc_ax,
-    out1, in1, out2, in2, rv, zf, zh, zl, ns_send, ns_recv, ew_send, ew_recv, co_recv, dep, fld,
-    ag_ssem, ag_rsem, ret_sem, a1_sem, halo_ssem, halo_rsem, a2_sem,
+    out1, in1, out2, in2, rv, zh, zl, ns_send, ns_recv, ew_send, ew_recv, co_recv, dep, fld,
+    load_sem, store_sem, ag_ssem, ag_rsem, ret_sem, a1_sem, halo_ssem, halo_rsem, a2_sem,
 ):
     row = lax.axis_index("row")
     col = lax.axis_index("col")
@@ -97,36 +98,51 @@
     def before(kr, kc):
         return lax.rem(row + (N_ROW - kr), N_ROW), lax.rem(col + (N_COL - kc), N_COL)
 
+    segments = [
+        (4, lambda i: 0, lambda i: 4 + i, True),
+        (8, lambda i: 2, lambda i: i, True),
+        (7, lambda i: 4, lambda i: 1 + i, True),
+        (32, lambda i: 3 - 2 * (i // N_COL), lambda i: lax.rem(i, N_COL), True),
+        (8, lambda i: 2, lambda i: 8 + i, True),
+        (3, lambda i: 0, lambda i: 3 - i, True),
+        (3, lambda i: 4 * ((i + 1) // 2), lambda i: 8 * (1 - i // 2), False),
+    ]
+
+    def over(segment, body):
+        count, kr, kc, _ = segment
+
+        def one(i, carry):
+            body(kr(i), kc(i))
+            return carry
+
+        lax.fori_loop(0, count, one, 0)
+
     def each_shift(body):
-        def first(i, carry):
-            body(0, 1 + i, True)
-            return carry
-
-        def middle(i, carry):
-            body(1 + i // N_COL, lax.rem(i, N_COL), True)
-            return carry
-
-        def last(i, carry):
-            body(4, 1 + i, True)
-            return carry
-
-        def alone(i, carry):
-            body(4 * lax.rem(i, 2), 8 * (1 - i // 2), False)
-            return carry
-
-        lax.fori_loop(0, 7, first, 0)
-        lax.fori_loop(0, 48, middle, 0)
-        lax.fori_loop(0, 7, last, 0)
-        lax.fori_loop(0, 2, alone, 0)
-        body(4, 0, False)
-
+        for segment in segments:
+            over(segment, body)
+
+    loads = [
+        pltpu.make_async_copy(source, target, load_sem.at[i])
+        for i, (source, target) in enumerate(
+            (
+                (btile_hbm, btile_ref),
+                (cells_hbm, cells_ref),
+                (offs_hbm, offs_ref),
+                (stren_hbm, stren_ref),
+            )
+        )
+    ]
+    for load in loads:
+        load.start()
     barrier = pltpu.get_barrier_semaphore()
 
-    def greet(kr, kc, _):
+    def greet(kr, kc):
         pl.semaphore_signal(barrier, inc=1, device_id=at(kr, kc), device_id_type=MESH)
 
     each_shift(greet)
 
+    for load in loads:
+        load.wait()
     widen = (iota((64, CYC), 1) // 2 == iota((64, CYC), 0)).astype(F32)
     tile_of = dot(
         jnp.broadcast_to(btile_ref[...].astype(F32), (8, 64)), widen, ((1,), (0,)), HIGH
@@ -144,20 +160,6 @@
     src[1:2] = pos_z
     src[2:3] = (STEP_LENGTH * 0.5) * strength
     src[3:4] = jnp.zeros((1, CYC), F32)
-
-    pl.semaphore_wait(barrier, 65)
-
-    def send_source(kr, kc, _):
-        pltpu.make_async_remote_copy(
-            src_ref=src,
-            dst_ref=ag.at[kr, kc],
-            send_sem=ag_ssem,
-            recv_sem=ag_rsem.at[kr, kc],
-            device_id=before(kr, kc),
-            device_id_type=MESH,
-        ).start()
-
-    each_shift(send_source)
 
     def column(v):
         return jnp.transpose(jnp.broadcast_to(v, (CYC, CYC)))
@@ -190,27 +192,6 @@
 
     block(src)
 
-    def meet(kr, kc, both):
-        pltpu.make_async_copy(src, ag.at[kr, kc], ag_rsem.at[kr, kc]).wait()
-        back_rad, back_ax = block(ag.at[kr, kc])
-        if both:
-            ret_send[kr, kc, 0:1] = jnp.sum(back_rad, axis=0, keepdims=True)
-            ret_send[kr, kc, 1:2] = jnp.sum(back_ax, axis=0, keepdims=True)
-            pltpu.make_async_remote_copy(
-                src_ref=ret_send.at[kr, kc],
-                dst_ref=ret_recv.at[kr, kc],
-                send_sem=ret_sem.at[0],
-                recv_sem=ret_sem.at[1],
-                device_id=at(kr, kc),
-                device_id_type=MESH,
-            ).start()
-
-    each_shift(meet)
-
-    def wait_bytes(ref, count, sem):
-        view = ref.at[pl.ds(0, count)]
-        pltpu.make_async_copy(view, view, sem).wait()
-
     lane = iota((CYC, CYC), 1)
     sub = iota((CYC, CYC), 0)
     tile_rows = jnp.broadcast_to(tile_of, (CYC, CYC))
@@ -218,6 +199,53 @@
     rank = jnp.sum(same.astype(F32), axis=0, keepdims=True)
     slot = rank.astype(jnp.int32) + (iota((1, CYC), 1) & 1)
     route = (sub == jnp.broadcast_to(tile_row, (CYC, CYC))).astype(F32)
+
+    pl.semaphore_wait(barrier, 65)
+
+    def send_source(kr, kc):
+        pltpu.make_async_remote_copy(
+            src_ref=src,
+            dst_ref=ag.at[kr, kc],
+            send_sem=ag_ssem,
+            recv_sem=ag_rsem.at[kr, kc],
+            device_id=before(kr, kc),
+            device_id_type=MESH,
+        ).start()
+
+    each_shift(send_source)
+
+    def arrive(kr, kc):
+        pltpu.make_async_copy(src, ag.at[kr, kc], ag_rsem.at[kr, kc]).wait()
+
+    def meet(kr, kc):
+        back_rad, back_ax = block(ag.at[kr, kc])
+        ret_send[kr, kc, 0:1] = jnp.sum(back_rad, axis=0, keepdims=True)
+        ret_send[kr, kc, 1:2] = jnp.sum(back_ax, axis=0, keepdims=True)
+
+    def send_back(kr, kc):
+        pltpu.make_async_remote_copy(
+            src_ref=ret_send.at[kr, kc],
+            dst_ref=ret_recv.at[kr, kc],
+            send_sem=ret_sem.at[0],
+            recv_sem=ret_sem.at[1],
+            device_id=at(kr, kc),
+            device_id_type=MESH,
+        ).start()
+
+    def arrive_meet(kr, kc):
+        arrive(kr, kc)
+        meet(kr, kc)
+
+    def full_meet(kr, kc):
+        arrive_meet(kr, kc)
+        send_back(kr, kc)
+
+    for segment in segments:
+        over(segment, full_meet if segment[-1] else arrive_meet)
+
+    def wait_bytes(ref, count, sem):
+        view = ref.at[pl.ds(0, count)]
+        pltpu.make_async_copy(view, view, sem).wait()
 
     own_rad = jnp.sum(jnp.transpose(acc_rad[...]), axis=0, keepdims=True)
     own_ax = jnp.sum(jnp.transpose(acc_ax[...]), axis=0, keepdims=True)
@@ -230,6 +258,8 @@
     disp_z = own_ax + got[1:2]
     disp_ref[0:1] = disp_r
     disp_ref[1:2] = disp_z
+    stores = [pltpu.make_async_copy(disp_ref, disp_out, store_sem.at[0])]
+    stores[0].start()
 
     moved_r = jnp.clip(offs[0:1] + disp_r, -1.0, 2.0)
     moved_z = jnp.clip(offs[1:2] + disp_z, -1.0, 2.0)
@@ -244,7 +274,8 @@
     me = row * N_COL + col
 
     def to_all(out, into, sem):
-        def outer(kr, carry):
+        def outer(i, carry):
+            kr = lax.rem(3 * i + 3, N_ROW)
             dr = lax.rem(row + kr, N_ROW)
 
             def send(dc):
@@ -415,8 +446,10 @@
         )
         new = here + VISCOSITY * laplace
         fld[8 * i : 8 * i + 8] = new
-        if i < CR // 8:
-            diff_ref[8 * i : 8 * i + 8] = new[:, 0:CZ]
+
+    tile = fld.at[pl.ds(0, CR), pl.ds(0, CZ)]
+    stores.append(pltpu.make_async_copy(tile, diff_out, store_sem.at[1]))
+    stores[1].start()
 
     read = dot3(halves(fld[...]), (zh[...], zl[...]), ((1,), (1,)))
     found = jnp.sum(read * radial[:EXT_R], axis=0, keepdims=True)
@@ -431,6 +464,9 @@
         jnp.where(iota((8, CYC), 0) == slot, mine, 0.0), axis=0, keepdims=True
     )
 
+    stores.append(pltpu.make_async_copy(renew_ref, renew_out, store_sem.at[2]))
+    stores[2].start()
+
     sent = ag.reshape(5 * N_COL, 4, CYC)
     wait_bytes(sent, 65, ag_ssem)
     wait_bytes(flat, 62, ret_sem.at[0])
@@ -438,21 +474,45 @@
     wait_bytes(out2, DEVICES - 1, a2_sem.at[0])
     for copy in copies:
         copy.wait_send()
+    for store in stores:
+        store.wait()
+
+
+def write_out(disp_ref, diff_ref, renew_ref, disp_out, diff_out, renew_out, sem):
+    pairs = [(disp_ref, disp_out), (renew_ref, renew_out)]
+    for i in range(8):
+        rows = pl.ds(i * CR // 8, CR // 8)
+        pairs.append((diff_ref.at[rows], diff_out.at[rows]))
+    copies = [
+        pltpu.make_async_copy(source, target, sem.at[i])
+        for i, (source, target) in enumerate(pairs)
+    ]
+    for copy in copies:
+        copy.start()
+    for copy in copies:
+        copy.wait()
 
 
 def on_device(cycle_cells, cycle_offsets, cycle_strength, block_tile):
-    vmem = pl.BlockSpec(memory_space=pltpu.VMEM)
+    hbm = pl.BlockSpec(memory_space=pl.ANY)
     dma = pltpu.SemaphoreType.DMA
-    displacement, diffused, renewed = pl.pallas_call(
+    shapes = [
+        jax.ShapeDtypeStruct((2, CYC), F32),
+        jax.ShapeDtypeStruct((CR, CZ), F32),
+        jax.ShapeDtypeStruct((1, CYC), F32),
+    ]
+    results = pl.pallas_call(
         kernel,
-        out_shape=[
-            jax.ShapeDtypeStruct((2, CYC), F32),
-            jax.ShapeDtypeStruct((CR, CZ), F32),
-            jax.ShapeDtypeStruct((1, CYC), F32),
-        ],
-        in_specs=[vmem] * 4,
-        out_specs=[vmem] * 3,
+        out_shape=shapes,
+        in_specs=[hbm] * 4,
+        out_specs=[hbm] * 3,
         scratch_shapes=[
+            pltpu.VMEM((2, CYC), jnp.int32),
+            pltpu.VMEM((2, CYC), F32),
+            pltpu.VMEM((1, CYC), F32),
+            pltpu.VMEM((1, 64), jnp.int32),
+            pltpu.VMEM((2, CYC), F32),
+            pltpu.VMEM((1, CYC), F32),
             pltpu.VMEM((4, CYC), F32),
             pltpu.VMEM((5, N_COL, 4, CYC), F32),
             pltpu.VMEM((5, N_COL, 2, CYC), F32),
@@ -468,7 +528,6 @@
             pltpu.VMEM((DEVICES, 1, CYC), F32),
             pltpu.VMEM((DEVICES, 1, CYC), F32),
             pltpu.VMEM((CYC, CYC), F32),
-            pltpu.VMEM((8, 128), F32),
             pltpu.VMEM((SLOTS, EXT_Z), BF16),
             pltpu.VMEM((SLOTS, EXT_Z), BF16),
             pltpu.VMEM((2, 8, EXT_Z), F32),
@@ -478,6 +537,8 @@
             pltpu.VMEM((4, 8, 128), F32),
             pltpu.VMEM((EXT_R, EXT_Z), F32),
             pltpu.VMEM((EXT_R, EXT_Z), F32),
+            dma((4,)),
+            dma((3,)),
             dma,
             dma((5, N_COL)),
             dma((2,)),
@@ -487,9 +548,17 @@
             dma((2,)),
         ],
         compiler_params=pltpu.CompilerParams(
-            collective_id=0, has_side_effects=True, vmem_limit_bytes=48 * 2**20
+            collective_id=0, has_side_effects=True, vmem_limit_bytes=40 * 2**20
         ),
     )(cycle_cells, cycle_offsets, cycle_strength.reshape(1, CYC), block_tile.reshape(1, -1))
+    displacement, diffused, renewed = pl.pallas_call(
+        write_out,
+        out_shape=shapes,
+        in_specs=[pl.BlockSpec(memory_space=pltpu.VMEM)] * 3,
+        out_specs=[hbm] * 3,
+        scratch_shapes=[dma((10,))],
+        compiler_params=pltpu.CompilerParams(vmem_limit_bytes=2**20),
+    )(*results)
     return displacement, diffused, renewed.reshape(CYC)
 
 

time: 58.8 us -> 57 us (0.969)
  local copies, waits for them, and re-layouts: 2.73 us -> 0.68 us
    unnamed x11 -> x8, local copies, waits for them, and re-layouts: 2.73 us -> 0.68 us
    pallas_call x1 -> x2, Pallas kernels: 55.2 us -> 55.5 us  [the longest x1 54.5 us: on_device(): pl.pallas_call(kernel, out_shape=shapes, in_specs=[hbm] * 4, out_specs=[h...]
where the time goes in v2:
time: 57 us; the launch traced here: 56.9 us
  Pallas kernels  55.5 us (97%)
  local copies, waits for them, and re-layouts  0.68 us (1%)
  between operations  0.67 us (1%)
    pallas_call x1, Pallas kernels, on_device(): pl.pallas_call(kernel, out_shape=shapes, in_specs=[hbm] * 4, out_specs=[h...  54.5 us

profile of v2, /device:TPU:1, one launch (start us, length us, event | category | flops | bytes accessed | tf_op | source)
XLA Modules:
  0.0 56.9 jit_solution(1344017243233038081)
XLA Ops:
  0.6 0.0 copy-start.1
  0.6 0.0 copy-start.3
  0.7 0.0 copy-start
  0.7 0.0 copy-start.2
  0.7 0.6 %copy-done.1 = f32[2,128]{1,0:T(2,128)S(1)} copy-done((f32[2,128]{1,0:T(2,128)S(1)}, f32[2,128]{1,0:T(2,128)}, u32[]{:S(2)}) %copy-start.1) | copy-done | bytes 1048
  1.3 0.0 copy-done.3
  1.3 0.0 copy-done
  1.3 0.0 copy-done.2
  1.3 54.5 %shard_map.67 = (f32[2,128]{1,0:T(2,128)S(1)}, f32[256,1024]{1,0:T(8,128)S(1)}, f32[1,128]{1,0:T(1,128)S(1)}) custom-call(s32[2,128]{1,0:T(2,128)S(1)} %copy-done, f32[2,128]{1,0:T(2,128)S(1)} %copy-done.1, f32[1,128]{1,0:T(1,128)S(1)} %bitcast.3, s32[1,64]{1,0:T(1,128)S(1)} %bitcast.4), custom_call_target="tpu_custom_call" | custom-call | tf_op jit(solution)/shard_map/pallas_call | solution.py:504
  55.8 1.1 %shard_map.68 = (f32[2,128]{1,0:T(2,128)}, f32[256,1024]{1,0:T(8,128)}, f32[1,128]{1,0:T(1,128)}) custom-call(f32[2,128]{1,0:T(2,128)S(1)} %get-tuple-element.9.disp_ref, f32[256,1024]{1,0:T(8,128)S(1)} %get-tuple-element.10.diff_ref, f32[1,128]{1,0:T(1,128)S(1)} %get-tuple-element.11.renew_ref), custom_call_target="tpu_custom_call" | custom-call | tf_op jit(solution)/shard_map/pallas_call | solution.py:554
Async XLA Ops:
  0.6 0.7 %copy-start.1 = (f32[2,128]{1,0:T(2,128)S(1)}, f32[2,128]{1,0:T(2,128)}, u32[]{:S(2)}) copy-start(f32[2,128]{1,0:T(2,128)} %offs_hbm.1) | copy-start | bytes 3076
  0.6 0.7 %copy-start.3 = (s32[64]{0:T(128)S(1)}, s32[64]{0:T(128)}, u32[]{:S(2)}) copy-start(s32[64]{0:T(128)} %param.7) | copy-start | bytes 772
  0.7 0.7 %copy-start = (s32[2,128]{1,0:T(2,128)S(1)}, s32[2,128]{1,0:T(2,128)}, u32[]{:S(2)}) copy-start(s32[2,128]{1,0:T(2,128)} %cells_hbm.1) | copy-start | bytes 3076
  0.7 0.7 %copy-start.2 = (f32[128]{0:T(128)S(1)}, f32[128]{0:T(128)}, u32[]{:S(2)}) copy-start(f32[128]{0:T(128)} %param.6) | copy-start | bytes 1540

commit v3 on v2

--- a/solution.py
+++ b/solution.py
@@ -18,7 +18,6 @@
 CZ = 1024
 EXT_R = 264
 EXT_Z = 1152
-ROWS = 280
 SLOTS = 512
 VISCOSITY = 0.2
 CORE_SQUARE = 4.0
@@ -82,12 +81,11 @@
 
 
 def kernel(
-    cells_hbm, offs_hbm, stren_hbm, btile_hbm,
-    disp_out, diff_out, renew_out,
-    cells_ref, offs_ref, stren_ref, btile_ref, disp_ref, renew_ref,
+    cells_ref, offs_ref, stren_ref, btile_ref,
+    disp_ref, diff_ref, renew_ref,
     src, ag, ret_send, ret_recv, tr, tz, tg, trr, acc_rad, acc_ax,
-    out1, in1, out2, in2, rv, zh, zl, ns_send, ns_recv, ew_send, ew_recv, co_recv, dep, fld,
-    load_sem, store_sem, ag_ssem, ag_rsem, ret_sem, a1_sem, halo_ssem, halo_rsem, a2_sem,
+    out1, in1, out2, in2, zh, zl, ns_send, ns_recv, ew_send, ew_recv, co_send, co_recv, dep, fld,
+    ag_ssem, ag_rsem, ret_sem, a1_sem, halo_ssem, halo_rsem, a2_sem,
 ):
     row = lax.axis_index("row")
     col = lax.axis_index("col")
@@ -121,19 +119,6 @@
         for segment in segments:
             over(segment, body)
 
-    loads = [
-        pltpu.make_async_copy(source, target, load_sem.at[i])
-        for i, (source, target) in enumerate(
-            (
-                (btile_hbm, btile_ref),
-                (cells_hbm, cells_ref),
-                (offs_hbm, offs_ref),
-                (stren_hbm, stren_ref),
-            )
-        )
-    ]
-    for load in loads:
-        load.start()
     barrier = pltpu.get_barrier_semaphore()
 
     def greet(kr, kc):
@@ -141,8 +126,6 @@
 
     each_shift(greet)
 
-    for load in loads:
-        load.wait()
     widen = (iota((64, CYC), 1) // 2 == iota((64, CYC), 0)).astype(F32)
     tile_of = dot(
         jnp.broadcast_to(btile_ref[...].astype(F32), (8, 64)), widen, ((1,), (0,)), HIGH
@@ -258,8 +241,6 @@
     disp_z = own_ax + got[1:2]
     disp_ref[0:1] = disp_r
     disp_ref[1:2] = disp_z
-    stores = [pltpu.make_async_copy(disp_ref, disp_out, store_sem.at[0])]
-    stores[0].start()
 
     moved_r = jnp.clip(offs[0:1] + disp_r, -1.0, 2.0)
     moved_z = jnp.clip(offs[1:2] + disp_z, -1.0, 2.0)
@@ -303,36 +284,22 @@
 
     to_all(out1, in1, a1_sem)
 
-    rv[...] = in1[:, 0, :]
-    across = jnp.transpose(rv[...])
-    step = iota((ROWS, CYC), 0)
-    wrapped = (iota((ROWS, CYC), 0) & 7) - jnp.where((iota((ROWS, CYC), 0) & 7) < 4, 0, 8)
-    cell_of_row = jnp.where(
-        step < 260,
-        step,
-        jnp.where(step < 264, step - 264, jnp.where(step < 272, CR + wrapped, wrapped)),
-    ).astype(F32)
-    radial = []
-    for s in range(4):
-        radial.append(tent((cell_of_row - across[8 * s : 8 * s + 1]) - across[8 * s + 1 : 8 * s + 2]))
-    radial = jnp.concatenate(radial, axis=1)
-    power = jnp.concatenate([across[8 * s + 4 : 8 * s + 5] for s in range(4)], axis=1)
-    loaded = halves(radial * power)
-
-    edge = iota((16, CYC), 0) & 7
-    edge = edge - jnp.where(edge < 4, 0, 8) + jnp.where(iota((16, CYC), 0) < 8, CZ, 0)
-    edge = edge.astype(F32)
-    axial_edge = jnp.concatenate(
-        [
-            tent((edge - across[8 * s + 2 : 8 * s + 3]) - across[8 * s + 3 : 8 * s + 4])
-            for s in range(4)
-        ],
-        axis=1,
-    )
-    strips = dot3(halves(axial_edge), loaded, ((1,), (1,)))
-    ew_send[...] = jnp.zeros((2, 8, 384), F32)
-    ew_send[0, :, 0:ROWS] = strips[0:8]
-    ew_send[1, :, 0:ROWS] = strips[8:16]
+    across = jnp.transpose(in1[:, 0, :])
+
+    def spread(value):
+        return jnp.concatenate([across[8 * s + value : 8 * s + value + 1] for s in range(4)], axis=1)
+
+    cell_r4, moved_r4, cell_z4, moved_z4, power = (spread(v) for v in range(5))
+    wrapped = iota((16, SLOTS), 0) & 7
+    wrapped = wrapped - jnp.where(wrapped < 4, 0, 8)
+    first = iota((16, SLOTS), 0) < 8
+    edge_z = tent(((wrapped + jnp.where(first, CZ, 0)).astype(F32) - cell_z4) - moved_z4)
+    edge_r = tent(((wrapped + jnp.where(first, CR, 0)).astype(F32) - cell_r4) - moved_r4) * power
+    edge_z, edge_r = halves(edge_z), halves(edge_r)
+    corners = dot3(edge_z, edge_r, ((1,), (1,)))
+    corners = jnp.concatenate([corners, jnp.zeros((16, 112), F32)], axis=1)
+    co_send[0] = corners[0:8]
+    co_send[1] = corners[8:16]
 
     next_r, prev_r = lax.rem(row + 1, N_ROW), lax.rem(row + N_ROW - 1, N_ROW)
     next_c, prev_c = lax.rem(col + 1, N_COL), lax.rem(col + N_COL - 1, N_COL)
@@ -351,39 +318,40 @@
         copy.start()
         copies.append(copy)
 
+    give(co_send.at[0], co_recv.at[0], (next_r, next_c))
+    give(co_send.at[0], co_recv.at[1], (next_r, prev_c))
+    give(co_send.at[1], co_recv.at[2], (prev_r, next_c))
+    give(co_send.at[1], co_recv.at[3], (prev_r, prev_c))
+
+    step = iota((EXT_R, SLOTS), 0)
+    cell_of_row = jnp.where(step < 260, step, step - EXT_R).astype(F32)
+    radial = tent((cell_of_row - cell_r4) - moved_r4)
+    loaded_h, loaded_l = halves(radial * power)
+    strips = dot3(edge_z, (loaded_h, loaded_l), ((1,), (1,)))
+    strips = jnp.concatenate([strips, jnp.zeros((16, 384 - EXT_R), F32)], axis=1)
+    ew_send[0] = strips[0:8]
+    ew_send[1] = strips[8:16]
     give(ew_send.at[0], ew_recv.at[0], (next_r, col))
     give(ew_send.at[1], ew_recv.at[1], (prev_r, col))
-    give(ew_send.at[0, :, pl.ds(256, 128)], co_recv.at[0], (next_r, next_c))
-    give(ew_send.at[0, :, pl.ds(256, 128)], co_recv.at[1], (next_r, prev_c))
-    give(ew_send.at[1, :, pl.ds(256, 128)], co_recv.at[2], (prev_r, next_c))
-    give(ew_send.at[1, :, pl.ds(256, 128)], co_recv.at[3], (prev_r, prev_c))
-
-    cell_of_lane = iota((16, EXT_Z), 1)
-    cell_of_lane = jnp.where(cell_of_lane < 1088, cell_of_lane, cell_of_lane - EXT_Z).astype(F32)
-
-    for s in range(4):
-
-        def axial(i, carry):
-            rows = pl.ds(pl.multiple_of(i * 16, 16), 16)
-            into = pl.ds(pl.multiple_of(s * CYC + i * 16, 16), 16)
-            one = rv[rows, :]
-            w = tent((cell_of_lane - one[:, 8 * s + 2 : 8 * s + 3]) - one[:, 8 * s + 3 : 8 * s + 4])
-            high, low = halves(w)
-            zh[into] = high
-            zl[into] = low
-            return carry
-
-        lax.fori_loop(0, 8, axial, 0)
-
-    loaded_h, loaded_l = loaded
-    along = ((1,), (0,))
-    ends = dot3((loaded_h[EXT_R:], loaded_l[EXT_R:]), (zh[...], zl[...]), along)
-    ns_send[0] = ends[0:8]
-    ns_send[1] = ends[8:16]
+
+    def axial(i, carry):
+        start = jnp.where(i < 34, i * 32, i * 32 - EXT_Z)
+        cell = (iota((32, SLOTS), 0) + start).astype(F32)
+        high, low = halves(tent((cell - cell_z4) - moved_z4))
+        rows = pl.ds(pl.multiple_of(i * 32, 32), 32)
+        zh[rows] = high
+        zl[rows] = low
+        return carry
+
+    lax.fori_loop(0, EXT_Z // 32, axial, 0, unroll=1)
+    weights = (zh[...], zl[...])
+    loaded = tuple(jnp.concatenate(pair, axis=0) for pair in zip((loaded_h, loaded_l), edge_r))
+    both = dot3(loaded, weights, ((1,), (1,)))
+    ns_send[0] = both[EXT_R : EXT_R + 8]
+    ns_send[1] = both[EXT_R + 8 :]
     give(ns_send.at[0], ns_recv.at[0], (row, next_c))
     give(ns_send.at[1], ns_recv.at[1], (row, prev_c))
-
-    dep[...] = dot3((loaded_h[:EXT_R], loaded_l[:EXT_R]), (zh[...], zl[...]), along)
+    dep[...] = both[:EXT_R]
 
     for copy in copies:
         copy.wait_recv()
@@ -396,12 +364,12 @@
         wide = jnp.where(present, ew_recv[i], 0.0)
         first, second, third = wide[:, 0:128], wide[:, 128:256], wide[:, 256:384]
         third = jnp.where(strip_lane < 8, third, 0.0)
-        low = jnp.where(has_prev_c & present, pltpu.roll(co_recv[2 * i], 120, axis=1), 0.0)
+        low = jnp.where(has_prev_c & present, co_recv[2 * i], 0.0)
         high = jnp.where(has_next_c & present, co_recv[2 * i + 1], 0.0)
         first += jnp.where(strip_lane < 4, low, 0.0)
         third += jnp.where((strip_lane >= 4) & (strip_lane < 8), low, 0.0)
-        third += jnp.where(strip_lane < 4, pltpu.roll(high, 112, axis=1), 0.0)
-        second += jnp.where(strip_lane >= 124, pltpu.roll(high, 104, axis=1), 0.0)
+        third += jnp.where(strip_lane < 4, pltpu.roll(high, 120, axis=1), 0.0)
+        second += jnp.where(strip_lane >= 124, pltpu.roll(high, 112, axis=1), 0.0)
         wide = jnp.concatenate([first, second, third], axis=1)
         upper = iota((8, 384), 0) < 4
         wide = jnp.concatenate(
@@ -446,13 +414,11 @@
         )
         new = here + VISCOSITY * laplace
         fld[8 * i : 8 * i + 8] = new
-
-    tile = fld.at[pl.ds(0, CR), pl.ds(0, CZ)]
-    stores.append(pltpu.make_async_copy(tile, diff_out, store_sem.at[1]))
-    stores[1].start()
-
-    read = dot3(halves(fld[...]), (zh[...], zl[...]), ((1,), (1,)))
-    found = jnp.sum(read * radial[:EXT_R], axis=0, keepdims=True)
+        if i < CR // 8:
+            diff_ref[8 * i : 8 * i + 8] = new[:, 0:CZ]
+
+    read = dot3(halves(fld[...]), (zh[...], zl[...]), ((1,), (0,)))
+    found = jnp.sum(read * radial, axis=0, keepdims=True)
     found = jnp.concatenate(
         [found[:, CYC * s : CYC * s + CYC] for s in range(4)] + [jnp.zeros((124, CYC), F32)], axis=0
     )
@@ -464,9 +430,6 @@
         jnp.where(iota((8, CYC), 0) == slot, mine, 0.0), axis=0, keepdims=True
     )
 
-    stores.append(pltpu.make_async_copy(renew_ref, renew_out, store_sem.at[2]))
-    stores[2].start()
-
     sent = ag.reshape(5 * N_COL, 4, CYC)
     wait_bytes(sent, 65, ag_ssem)
     wait_bytes(flat, 62, ret_sem.at[0])
@@ -474,8 +437,6 @@
     wait_bytes(out2, DEVICES - 1, a2_sem.at[0])
     for copy in copies:
         copy.wait_send()
-    for store in stores:
-        store.wait()
 
 
 def write_out(disp_ref, diff_ref, renew_ref, disp_out, diff_out, renew_out, sem):
@@ -494,6 +455,7 @@
 
 
 def on_device(cycle_cells, cycle_offsets, cycle_strength, block_tile):
+    vmem = pl.BlockSpec(memory_space=pltpu.VMEM)
     hbm = pl.BlockSpec(memory_space=pl.ANY)
     dma = pltpu.SemaphoreType.DMA
     shapes = [
@@ -504,15 +466,9 @@
     results = pl.pallas_call(
         kernel,
         out_shape=shapes,
-        in_specs=[hbm] * 4,
-        out_specs=[hbm] * 3,
+        in_specs=[vmem] * 4,
+        out_specs=[vmem] * 3,
         scratch_shapes=[
-            pltpu.VMEM((2, CYC), jnp.int32),
-            pltpu.VMEM((2, CYC), F32),
-            pltpu.VMEM((1, CYC), F32),
-            pltpu.VMEM((1, 64), jnp.int32),
-            pltpu.VMEM((2, CYC), F32),
-            pltpu.VMEM((1, CYC), F32),
             pltpu.VMEM((4, CYC), F32),
             pltpu.VMEM((5, N_COL, 4, CYC), F32),
             pltpu.VMEM((5, N_COL, 2, CYC), F32),
@@ -527,18 +483,16 @@
             pltpu.VMEM((DEVICES, 1, CYC), F32),
             pltpu.VMEM((DEVICES, 1, CYC), F32),
             pltpu.VMEM((DEVICES, 1, CYC), F32),
-            pltpu.VMEM((CYC, CYC), F32),
-            pltpu.VMEM((SLOTS, EXT_Z), BF16),
-            pltpu.VMEM((SLOTS, EXT_Z), BF16),
+            pltpu.VMEM((EXT_Z, SLOTS), BF16),
+            pltpu.VMEM((EXT_Z, SLOTS), BF16),
             pltpu.VMEM((2, 8, EXT_Z), F32),
             pltpu.VMEM((2, 8, EXT_Z), F32),
             pltpu.VMEM((2, 8, 384), F32),
             pltpu.VMEM((2, 8, 384), F32),
+            pltpu.VMEM((2, 8, 128), F32),
             pltpu.VMEM((4, 8, 128), F32),
             pltpu.VMEM((EXT_R, EXT_Z), F32),
             pltpu.VMEM((EXT_R, EXT_Z), F32),
-            dma((4,)),
-            dma((3,)),
             dma,
             dma((5, N_COL)),
             dma((2,)),
@@ -554,7 +508,7 @@
     displacement, diffused, renewed = pl.pallas_call(
         write_out,
         out_shape=shapes,
-        in_specs=[pl.BlockSpec(memory_space=pltpu.VMEM)] * 3,
+        in_specs=[vmem] * 3,
         out_specs=[hbm] * 3,
         scratch_shapes=[dma((10,))],
         compiler_params=pltpu.CompilerParams(vmem_limit_bytes=2**20),

time: 57 us -> 56.1 us (0.984)
  Pallas kernels: 55.5 us -> 54.7 us
    pallas_call x2, Pallas kernels: 55.5 us -> 54.7 us  [the longest x1 53.6 us: on_device(): pl.pallas_call(kernel, out_shape=shapes, in_specs=[vmem] * 4, out_specs=[...]
where the time goes in v3:
time: 56.1 us; the launch traced here: 56 us
  Pallas kernels  54.7 us (98%)
  local copies, waits for them, and re-layouts  0.68 us (1%)
  between operations  0.67 us (1%)
    pallas_call x1, Pallas kernels, on_device(): pl.pallas_call(kernel, out_shape=shapes, in_specs=[vmem] * 4, out_specs=[...  53.6 us

profile of v3, /device:TPU:1, one launch (start us, length us, event | category | flops | bytes accessed | tf_op | source)
XLA Modules:
  0.0 56.0 jit_solution(7119438284766817828)
XLA Ops:
  0.6 0.0 copy-start.1
  0.6 0.0 copy-start.3
  0.7 0.0 copy-start
  0.7 0.0 copy-start.2
  0.7 0.6 %copy-done.1 = f32[2,128]{1,0:T(2,128)S(1)} copy-done((f32[2,128]{1,0:T(2,128)S(1)}, f32[2,128]{1,0:T(2,128)}, u32[]{:S(2)}) %copy-start.1) | copy-done | bytes 1048
  1.3 0.0 copy-done.3
  1.3 0.0 copy-done
  1.3 0.0 copy-done.2
  1.3 53.6 %shard_map.67 = (f32[2,128]{1,0:T(2,128)S(1)}, f32[256,1024]{1,0:T(8,128)S(1)}, f32[1,128]{1,0:T(1,128)S(1)}) custom-call(s32[2,128]{1,0:T(2,128)S(1)} %copy-done, f32[2,128]{1,0:T(2,128)S(1)} %copy-done.1, f32[1,128]{1,0:T(1,128)S(1)} %bitcast.3, s32[1,64]{1,0:T(1,128)S(1)} %bitcast.4), custom_call_target="tpu_custom_call" | custom-call | tf_op jit(solution)/shard_map/pallas_call | solution.py:466
  55.0 1.1 %shard_map.68 = (f32[2,128]{1,0:T(2,128)}, f32[256,1024]{1,0:T(8,128)}, f32[1,128]{1,0:T(1,128)}) custom-call(f32[2,128]{1,0:T(2,128)S(1)} %get-tuple-element.9.disp_ref, f32[256,1024]{1,0:T(8,128)S(1)} %get-tuple-element.10.diff_ref, f32[1,128]{1,0:T(1,128)S(1)} %get-tuple-element.11.renew_ref), custom_call_target="tpu_custom_call" | custom-call | tf_op jit(solution)/shard_map/pallas_call | solution.py:508
Async XLA Ops:
  0.6 0.7 %copy-start.1 = (f32[2,128]{1,0:T(2,128)S(1)}, f32[2,128]{1,0:T(2,128)}, u32[]{:S(2)}) copy-start(f32[2,128]{1,0:T(2,128)} %offs_ref.1) | copy-start | bytes 3076
  0.6 0.7 %copy-start.3 = (s32[64]{0:T(128)S(1)}, s32[64]{0:T(128)}, u32[]{:S(2)}) copy-start(s32[64]{0:T(128)} %param.7) | copy-start | bytes 772
  0.7 0.7 %copy-start = (s32[2,128]{1,0:T(2,128)S(1)}, s32[2,128]{1,0:T(2,128)}, u32[]{:S(2)}) copy-start(s32[2,128]{1,0:T(2,128)} %cells_ref.1) | copy-start | bytes 3076
  0.7 0.7 %copy-start.2 = (f32[128]{0:T(128)S(1)}, f32[128]{0:T(128)}, u32[]{:S(2)}) copy-start(f32[128]{0:T(128)} %param.6) | copy-start | bytes 1540

commit v4 on v3

--- a/solution.py
+++ b/solution.py
@@ -42,7 +42,9 @@
 
 def dot3(a, b, contract):
     (ah, al), (bh, bl) = a, b
-    return dot(ah, bh, contract) + (dot(ah, bl, contract) + dot(al, bh, contract))
+    ka, kb = contract[0][0], contract[1][0]
+    left = jnp.concatenate([ah, ah, al], axis=ka)
+    return dot(left, jnp.concatenate([bh, bl, bh], axis=kb), contract)
 
 
 def tent(x):

time: 56.1 us -> 54.1 us (0.964)
  Pallas kernels: 54.7 us -> 52.7 us
    pallas_call x1, Pallas kernels: 53.6 us -> 51.6 us  [on_device(): pl.pallas_call(kernel, out_shape=shapes, in_specs=[vmem] * 4, out_specs=[...]
where the time goes in v4:
time: 54.1 us; the launch traced here: 54 us
  Pallas kernels  52.7 us (97%)
  local copies, waits for them, and re-layouts  0.68 us (1%)
  between operations  0.67 us (1%)
    pallas_call x1, Pallas kernels, on_device(): pl.pallas_call(kernel, out_shape=shapes, in_specs=[vmem] * 4, out_specs=[...  51.6 us

profile of v4, /device:TPU:1, one launch (start us, length us, event | category | flops | bytes accessed | tf_op | source)
XLA Modules:
  0.0 54.0 jit_solution(12530713523941062086)
XLA Ops:
  0.6 0.0 copy-start.1
  0.6 0.0 copy-start.3
  0.7 0.0 copy-start
  0.7 0.0 copy-start.2
  0.7 0.6 %copy-done.1 = f32[2,128]{1,0:T(2,128)S(1)} copy-done((f32[2,128]{1,0:T(2,128)S(1)}, f32[2,128]{1,0:T(2,128)}, u32[]{:S(2)}) %copy-start.1) | copy-done | bytes 1048
  1.3 0.0 copy-done.3
  1.3 0.0 copy-done
  1.3 0.0 copy-done.2
  1.3 51.6 %shard_map.67 = (f32[2,128]{1,0:T(2,128)S(1)}, f32[256,1024]{1,0:T(8,128)S(1)}, f32[1,128]{1,0:T(1,128)S(1)}) custom-call(s32[2,128]{1,0:T(2,128)S(1)} %copy-done, f32[2,128]{1,0:T(2,128)S(1)} %copy-done.1, f32[1,128]{1,0:T(1,128)S(1)} %bitcast.3, s32[1,64]{1,0:T(1,128)S(1)} %bitcast.4), custom_call_target="tpu_custom_call" | custom-call | tf_op jit(solution)/shard_map/pallas_call | solution.py:468
  53.0 1.1 %shard_map.68 = (f32[2,128]{1,0:T(2,128)}, f32[256,1024]{1,0:T(8,128)}, f32[1,128]{1,0:T(1,128)}) custom-call(f32[2,128]{1,0:T(2,128)S(1)} %get-tuple-element.9.disp_ref, f32[256,1024]{1,0:T(8,128)S(1)} %get-tuple-element.10.diff_ref, f32[1,128]{1,0:T(1,128)S(1)} %get-tuple-element.11.renew_ref), custom_call_target="tpu_custom_call" | custom-call | tf_op jit(solution)/shard_map/pallas_call | solution.py:510
Async XLA Ops:
  0.6 0.7 %copy-start.1 = (f32[2,128]{1,0:T(2,128)S(1)}, f32[2,128]{1,0:T(2,128)}, u32[]{:S(2)}) copy-start(f32[2,128]{1,0:T(2,128)} %offs_ref.1) | copy-start | bytes 3076
  0.6 0.7 %copy-start.3 = (s32[64]{0:T(128)S(1)}, s32[64]{0:T(128)}, u32[]{:S(2)}) copy-start(s32[64]{0:T(128)} %param.7) | copy-start | bytes 772
  0.7 0.7 %copy-start = (s32[2,128]{1,0:T(2,128)S(1)}, s32[2,128]{1,0:T(2,128)}, u32[]{:S(2)}) copy-start(s32[2,128]{1,0:T(2,128)} %cells_ref.1) | copy-start | bytes 3076
  0.7 0.7 %copy-start.2 = (f32[128]{0:T(128)S(1)}, f32[128]{0:T(128)}, u32[]{:S(2)}) copy-start(f32[128]{0:T(128)} %param.6) | copy-start | bytes 1540

commit v5 on v4

--- a/solution.py
+++ b/solution.py
@@ -355,6 +355,39 @@
     give(ns_send.at[1], ns_recv.at[1], (row, prev_c))
     dep[...] = both[:EXT_R]
 
+    base = col * CR
+
+    def viscous(i, window, keep):
+        cut = (lambda x: x) if keep is None else (lambda x: x[:, keep[0] : keep[1]])
+        load = lambda k: window(pl.ds(8 * (k % (EXT_R // 8)), 8))
+        wide = load(i)
+        width = wide.shape[1]
+        here = cut(wide)
+        inward = jnp.concatenate([cut(load(i - 1))[7:8], here[0:7]], axis=0)
+        outward = jnp.concatenate([here[1:8], cut(load(i + 1))[0:1]], axis=0)
+        forward = cut(pltpu.roll(wide, width - 1, axis=1))
+        backward = cut(pltpu.roll(wide, 1, axis=1))
+        number = iota((8, 128), 0) + 8 * i
+        number = jnp.where(number < 260, number, number - EXT_R) + base
+        radius = jnp.maximum(number, 1).astype(F32)
+        count = here.shape[1] // 128
+        half = jnp.concatenate([0.5 / radius] * count, axis=1)
+        square = jnp.concatenate([1.0 / (radius * radius)] * count, axis=1)
+        laplace = (
+            (outward + inward)
+            + (forward + backward)
+            - 4.0 * here
+            + (outward - inward) * half
+            - here * square
+        )
+        return here + VISCOSITY * laplace
+
+    inner = range(1, CR // 8 - 1)
+    for i in inner:
+        new = viscous(i, lambda rows: dep[rows, 0:1024], (128, 896))
+        fld[8 * i : 8 * i + 8, 128:896] = new
+        diff_ref[8 * i : 8 * i + 8, 128:896] = new
+
     for copy in copies:
         copy.wait_recv()
 
@@ -393,31 +426,21 @@
     dep[248:256] += jnp.where(upper, 0.0, below)
     dep[256:264] += jnp.where(upper, below, above)
 
-    base = col * CR
-    for i in range(EXT_R // 8):
-        here = dep[8 * i : 8 * i + 8]
-        prev = dep[8 * i - 8 : 8 * i] if i else dep[EXT_R - 8 : EXT_R]
-        nxt = dep[8 * i + 8 : 8 * i + 16] if i < EXT_R // 8 - 1 else dep[0:8]
-        inward = jnp.concatenate([prev[7:8], here[0:7]], axis=0)
-        outward = jnp.concatenate([here[1:8], nxt[0:1]], axis=0)
-        forward = pltpu.roll(here, EXT_Z - 1, axis=1)
-        backward = pltpu.roll(here, 1, axis=1)
-        number = iota((8, 128), 0) + 8 * i
-        number = jnp.where(number < 260, number, number - EXT_R) + base
-        radius = jnp.maximum(number, 1).astype(F32)
-        half = jnp.concatenate([0.5 / radius] * 9, axis=1)
-        square = jnp.concatenate([1.0 / (radius * radius)] * 9, axis=1)
-        laplace = (
-            (outward + inward)
-            + (forward + backward)
-            - 4.0 * here
-            + (outward - inward) * half
-            - here * square
-        )
-        new = here + VISCOSITY * laplace
+    for i in (0, CR // 8 - 1, CR // 8):
+        new = viscous(i, lambda rows: dep[rows], None)
         fld[8 * i : 8 * i + 8] = new
         if i < CR // 8:
             diff_ref[8 * i : 8 * i + 8] = new[:, 0:CZ]
+    for i in inner:
+        new = viscous(
+            i,
+            lambda rows: jnp.concatenate([dep[rows, 768:1152], dep[rows, 0:256]], axis=1),
+            (128, 512),
+        )
+        fld[8 * i : 8 * i + 8, 896:1152] = new[:, 0:256]
+        fld[8 * i : 8 * i + 8, 0:128] = new[:, 256:384]
+        diff_ref[8 * i : 8 * i + 8, 896:1024] = new[:, 0:128]
+        diff_ref[8 * i : 8 * i + 8, 0:128] = new[:, 256:384]
 
     read = dot3(halves(fld[...]), (zh[...], zl[...]), ((1,), (0,)))
     found = jnp.sum(read * radial, axis=0, keepdims=True)

time: 54.1 us -> 53.9 us (level)
  no operation moved by 1% of the time
where the time goes in v5:
time: 53.9 us; the launch traced here: 53.8 us
  Pallas kernels  52.4 us (97%)
  local copies, waits for them, and re-layouts  0.68 us (1%)
  between operations  0.67 us (1%)
    pallas_call x1, Pallas kernels, on_device(): pl.pallas_call(kernel, out_shape=shapes, in_specs=[vmem] * 4, out_specs=[...  51.4 us

profile of v5, /device:TPU:1, one launch (start us, length us, event | category | flops | bytes accessed | tf_op | source)
XLA Modules:
  0.0 53.8 jit_solution(8146694128519898660)
XLA Ops:
  0.6 0.0 copy-start.1
  0.6 0.0 copy-start.3
  0.7 0.0 copy-start
  0.7 0.0 copy-start.2
  0.7 0.6 %copy-done.1 = f32[2,128]{1,0:T(2,128)S(1)} copy-done((f32[2,128]{1,0:T(2,128)S(1)}, f32[2,128]{1,0:T(2,128)}, u32[]{:S(2)}) %copy-start.1) | copy-done | bytes 1048
  1.3 0.0 copy-done.3
  1.3 0.0 copy-done
  1.3 0.0 copy-done.2
  1.3 51.4 %shard_map.67 = (f32[2,128]{1,0:T(2,128)S(1)}, f32[256,1024]{1,0:T(8,128)S(1)}, f32[1,128]{1,0:T(1,128)S(1)}) custom-call(s32[2,128]{1,0:T(2,128)S(1)} %copy-done, f32[2,128]{1,0:T(2,128)S(1)} %copy-done.1, f32[1,128]{1,0:T(1,128)S(1)} %bitcast.3, s32[1,64]{1,0:T(1,128)S(1)} %bitcast.4), custom_call_target="tpu_custom_call" | custom-call | tf_op jit(solution)/shard_map/pallas_call | solution.py:491
  52.7 1.1 %shard_map.68 = (f32[2,128]{1,0:T(2,128)}, f32[256,1024]{1,0:T(8,128)}, f32[1,128]{1,0:T(1,128)}) custom-call(f32[2,128]{1,0:T(2,128)S(1)} %get-tuple-element.9.disp_ref, f32[256,1024]{1,0:T(8,128)S(1)} %get-tuple-element.10.diff_ref, f32[1,128]{1,0:T(1,128)S(1)} %get-tuple-element.11.renew_ref), custom_call_target="tpu_custom_call" | custom-call | tf_op jit(solution)/shard_map/pallas_call | solution.py:533
Async XLA Ops:
  0.6 0.7 %copy-start.1 = (f32[2,128]{1,0:T(2,128)S(1)}, f32[2,128]{1,0:T(2,128)}, u32[]{:S(2)}) copy-start(f32[2,128]{1,0:T(2,128)} %offs_ref.1) | copy-start | bytes 3076
  0.6 0.7 %copy-start.3 = (s32[64]{0:T(128)S(1)}, s32[64]{0:T(128)}, u32[]{:S(2)}) copy-start(s32[64]{0:T(128)} %param.7) | copy-start | bytes 772
  0.7 0.7 %copy-start = (s32[2,128]{1,0:T(2,128)S(1)}, s32[2,128]{1,0:T(2,128)}, u32[]{:S(2)}) copy-start(s32[2,128]{1,0:T(2,128)} %cells_ref.1) | copy-start | bytes 3076
  0.7 0.7 %copy-start.2 = (f32[128]{0:T(128)S(1)}, f32[128]{0:T(128)}, u32[]{:S(2)}) copy-start(f32[128]{0:T(128)} %param.6) | copy-start | bytes 1540

commit v6 on v5

--- a/solution.py
+++ b/solution.py
@@ -126,7 +126,8 @@
     def greet(kr, kc):
         pl.semaphore_signal(barrier, inc=1, device_id=at(kr, kc), device_id_type=MESH)
 
-    each_shift(greet)
+    for segment in reversed(segments):
+        over(segment, greet)
 
     widen = (iota((64, CYC), 1) // 2 == iota((64, CYC), 0)).astype(F32)
     tile_of = dot(
@@ -251,8 +252,9 @@
     blank = jnp.zeros((3, CYC), F32)
     values = jnp.concatenate([local_r, moved_r, local_z, moved_z, strength, blank], axis=0)
     payload = jnp.concatenate([jnp.where(slot == s, values, 0.0) for s in range(4)], axis=0)
-    payload = jnp.concatenate([payload, jnp.zeros((96, CYC), F32)], axis=0)
-    out1[:, 0, :] = dot(route, payload, ((1,), (1,)), HIGH)
+    out1[:, 0, :] = jnp.concatenate(
+        [dot(route, payload, ((1,), (1,)), HIGH), jnp.zeros((CYC, 96), F32)], axis=1
+    )
 
     me = row * N_COL + col
 
@@ -466,8 +468,8 @@
 
 def write_out(disp_ref, diff_ref, renew_ref, disp_out, diff_out, renew_out, sem):
     pairs = [(disp_ref, disp_out), (renew_ref, renew_out)]
-    for i in range(8):
-        rows = pl.ds(i * CR // 8, CR // 8)
+    for i in range(2):
+        rows = pl.ds(i * CR // 2, CR // 2)
         pairs.append((diff_ref.at[rows], diff_out.at[rows]))
     copies = [
         pltpu.make_async_copy(source, target, sem.at[i])
@@ -535,7 +537,7 @@
         out_shape=shapes,
         in_specs=[vmem] * 3,
         out_specs=[hbm] * 3,
-        scratch_shapes=[dma((10,))],
+        scratch_shapes=[dma((4,))],
         compiler_params=pltpu.CompilerParams(vmem_limit_bytes=2**20),
     )(*results)
     return displacement, diffused, renewed.reshape(CYC)

time: 53.9 us -> 53.9 us (level)
  no operation moved by 1% of the time
where the time goes in v6:
time: 53.9 us; the launch traced here: 53.7 us
  Pallas kernels  52.4 us (97%)
  local copies, waits for them, and re-layouts  0.68 us (1%)
  between operations  0.67 us (1%)
    pallas_call x1, Pallas kernels, on_device(): pl.pallas_call(kernel, out_shape=shapes, in_specs=[vmem] * 4, out_specs=[...  51.4 us

profile of v6, /device:TPU:1, one launch (start us, length us, event | category | flops | bytes accessed | tf_op | source)
XLA Modules:
  0.0 53.7 jit_solution(1162151483905836659)
XLA Ops:
  0.6 0.0 copy-start.1
  0.6 0.0 copy-start.3
  0.7 0.0 copy-start
  0.7 0.0 copy-start.2
  0.7 0.6 %copy-done.1 = f32[2,128]{1,0:T(2,128)S(1)} copy-done((f32[2,128]{1,0:T(2,128)S(1)}, f32[2,128]{1,0:T(2,128)}, u32[]{:S(2)}) %copy-start.1) | copy-done | bytes 1048
  1.3 0.0 copy-done.3
  1.3 0.0 copy-done
  1.3 0.0 copy-done.2
  1.3 51.4 %shard_map.67 = (f32[2,128]{1,0:T(2,128)S(1)}, f32[256,1024]{1,0:T(8,128)S(1)}, f32[1,128]{1,0:T(1,128)S(1)}) custom-call(s32[2,128]{1,0:T(2,128)S(1)} %copy-done, f32[2,128]{1,0:T(2,128)S(1)} %copy-done.1, f32[1,128]{1,0:T(1,128)S(1)} %bitcast.3, s32[1,64]{1,0:T(1,128)S(1)} %bitcast.4), custom_call_target="tpu_custom_call" | custom-call | tf_op jit(solution)/shard_map/pallas_call | solution.py:493
  52.7 1.0 %shard_map.68 = (f32[2,128]{1,0:T(2,128)}, f32[256,1024]{1,0:T(8,128)}, f32[1,128]{1,0:T(1,128)}) custom-call(f32[2,128]{1,0:T(2,128)S(1)} %get-tuple-element.9.disp_ref, f32[256,1024]{1,0:T(8,128)S(1)} %get-tuple-element.10.diff_ref, f32[1,128]{1,0:T(1,128)S(1)} %get-tuple-element.11.renew_ref), custom_call_target="tpu_custom_call" | custom-call | tf_op jit(solution)/shard_map/pallas_call | solution.py:535
Async XLA Ops:
  0.6 0.7 %copy-start.1 = (f32[2,128]{1,0:T(2,128)S(1)}, f32[2,128]{1,0:T(2,128)}, u32[]{:S(2)}) copy-start(f32[2,128]{1,0:T(2,128)} %offs_ref.1) | copy-start | bytes 3076
  0.6 0.7 %copy-start.3 = (s32[64]{0:T(128)S(1)}, s32[64]{0:T(128)}, u32[]{:S(2)}) copy-start(s32[64]{0:T(128)} %param.7) | copy-start | bytes 772
  0.7 0.7 %copy-start = (s32[2,128]{1,0:T(2,128)S(1)}, s32[2,128]{1,0:T(2,128)}, u32[]{:S(2)}) copy-start(s32[2,128]{1,0:T(2,128)} %cells_ref.1) | copy-start | bytes 3076
  0.7 0.7 %copy-start.2 = (f32[128]{0:T(128)S(1)}, f32[128]{0:T(128)}, u32[]{:S(2)}) copy-start(f32[128]{0:T(128)} %param.6) | copy-start | bytes 1540
